TPU v7x, 256 devices: a whole 4x4x8 slice. The times are simulated.
256 devices in a mesh: dp: 32 (over x, y, core), rep: 8 (over z).
Axes of the slice: x: 4, y: 4, z: 8, core: 2. Of those that a mesh axis runs over, the one named last changes fastest.
Arguments:
- cache: bfloat16 [2048, 64, 576], P(('rep', 'dp')), parts along dimension 0, may hold values from -6 to 6
- lengths: int32 [2048], P(('rep', 'dp')), parts along dimension 0, may hold values from 2 to 62
- queries: bfloat16 [2048, 2, 64, 576], P(('rep', 'dp')), parts along dimension 0, may hold values from -4 to 4
- fresh: bfloat16 [2048, 2, 576], P(('rep', 'dp')), parts along dimension 0, may hold values from -6 to 6
- w_uv: bfloat16 [64, 512, 128], P('dp'), may hold values from -0.25 to 0.25
- w_out: bfloat16 [8192, 7168], P('dp'), may hold values from -0.0625 to 0.0625
- outgoing: int32 [1024], P(('rep', 'dp')), parts along dimension 0, may hold values from 0 to 7, as said below
- targets: int32 [1024], P(('rep', 'dp')), parts along dimension 0, may hold values from 0 to 31, as said below
Outputs:
- new_cache: bfloat16 [2048, 64, 576], P(('rep', 'dp')), parts along dimension 0
- attended: bfloat16 [2048, 2, 7168], P(('rep', 'dp')), parts along dimension 0
There are 8 independent parts, one for each index of `rep`. A program takes and returns all parts, laid end to end along the dimension named above; an argument that names none is the same for every part. Nothing has to cross between parts.
Inputs may be any that keep to these rules, and one draw needn't show every extreme that they name: `outgoing`: the 4 slots listed for one device are different. `targets`: the 4 rows of one device go to 4 different other devices, and every device receives exactly 4 rows.
All inputs are finite; a program needn't handle non-finite values.
Results may differ from a plain program's by a relative error of at most 0.019.
Values may be sent and summed in bfloat16 or wider, within the bound.
A program may use at most 64 MiB of HBM per device.

v0:
```python
import math

import jax
import jax.numpy as jnp
from jax import lax
from jax.sharding import PartitionSpec as P

ROPE = 64
VD = 128


def place_rows(members, outgoing, targets, peers):
    dest = jnp.arange(peers, dtype=jnp.int32)
    match = targets[None, :] == dest[:, None]
    present = jnp.any(match, axis=1)
    source_slot = jnp.sum(jnp.where(match, outgoing[None, :], 0), axis=1)
    placed = []
    for member in members:
        picked = member[source_slot]
        shaped = present.reshape((peers,) + (1,) * (member.ndim - 1))
        placed.append(jnp.where(shaped, picked, jnp.zeros((), member.dtype)))
    return placed


def take_first(members, present, count):
    rank = jnp.cumsum(present.astype(jnp.int32)) - 1
    wanted = jnp.arange(count, dtype=jnp.int32)
    hit = present[None, :] & (rank[None, :] == wanted[:, None])
    anchor = jnp.arange(present.shape[0], dtype=jnp.int32)
    source = jnp.sum(jnp.where(hit, anchor[None, :], 0), axis=1)
    return [member[source] for member in members]


def regroup(local, arrived, present, outgoing):
    row_count = local[0].shape[0]
    moving = outgoing.shape[0]
    slots = jnp.arange(row_count, dtype=jnp.int32)
    staying = jnp.logical_not(jnp.any(slots[:, None] == outgoing[None, :], axis=1))
    kept = take_first(local, staying, row_count - moving)
    received = take_first(arrived, present, moving)
    return [jnp.concatenate([first, second], axis=0) for first, second in zip(kept, received)]


def decode(cache, lengths, queries, fresh, w_uv, w_out):
    row_count, slot_count, entry = cache.shape
    step_count = fresh.shape[1]
    head_count = queries.shape[2]
    latent_width = w_uv.shape[1]
    slots = jnp.arange(slot_count, dtype=jnp.int32)
    updated = cache
    for step in range(step_count):
        spot = (slots[None, :] == (lengths + step)[:, None])[:, :, None]
        updated = jnp.where(spot, fresh[:, step][:, None, :], updated)
    scale = 1.0 / math.sqrt(VD + ROPE)
    flat_q = queries.reshape(row_count, step_count * head_count, entry)
    scores = jnp.einsum("rqc,rkc->rqk", flat_q, updated, preferred_element_type=jnp.float32) * scale
    step_of = jnp.repeat(jnp.arange(step_count, dtype=jnp.int32), head_count)
    limit = lengths[:, None] + step_of[None, :]
    allowed = slots[None, None, :] <= limit[:, :, None]
    scores = jnp.where(allowed, scores, -1e30)
    top = jnp.max(scores, axis=2, keepdims=True)
    weights = jnp.exp(scores - top)
    probs = (weights / jnp.sum(weights, axis=2, keepdims=True)).astype(jnp.bfloat16)
    latent = jnp.einsum(
        "rqk,rkl->rql", probs, updated[:, :, :latent_width], preferred_element_type=jnp.float32
    )
    latent = latent.astype(jnp.bfloat16).reshape(row_count, step_count, head_count, latent_width)
    mixed = lax.all_to_all(latent, "dp", split_axis=2, concat_axis=0, tiled=True)
    values = jnp.einsum("rshl,hlv->rshv", mixed, w_uv, preferred_element_type=jnp.float32).astype(
        jnp.bfloat16
    )
    flat_v = values.reshape(values.shape[0] * step_count, -1)
    sums = lax.psum_scatter(
        jnp.dot(flat_v, w_out, preferred_element_type=jnp.float32).astype(jnp.bfloat16),
        "dp",
        scatter_dimension=0,
        tiled=True,
    )
    attended = sums.reshape(row_count, step_count, w_out.shape[1])
    return (updated, attended)


def per_device(cache, lengths, queries, fresh, w_uv, w_out, outgoing, targets):
    peers = lax.axis_size("dp")
    updated, attended = decode(cache, lengths, queries, fresh, w_uv, w_out)
    sent = place_rows([updated, lengths, attended], outgoing, targets, peers)
    arrived = (
        lax.all_to_all(sent[0], "dp", split_axis=0, concat_axis=0, tiled=True),
        lax.all_to_all(sent[1], "dp", split_axis=0, concat_axis=0, tiled=True),
        lax.all_to_all(sent[2], "dp", split_axis=0, concat_axis=0, tiled=True),
    )
    present = arrived[1] > 0
    moved_rows = regroup([updated, lengths, attended], list(arrived), present, outgoing)
    return (moved_rows[0], moved_rows[2])


def solution(mesh):
    in_specs = (
        P(("rep", "dp"), None, None),
        P(("rep", "dp")),
        P(("rep", "dp"), None, None, None),
        P(("rep", "dp"), None, None),
        P("dp", None, None),
        P("dp", None),
        P(("rep", "dp")),
        P(("rep", "dp")),
    )
    out_specs = (P(("rep", "dp"), None, None), P(("rep", "dp"), None, None))
    return jax.shard_map(
        per_device, mesh=mesh, in_specs=in_specs, out_specs=out_specs, check_vma=False
    )
```

profile of v0, /device:TPU:1, one launch (start us, length us, event | category | flops | bytes accessed | tf_op | source)
XLA Modules:
  0.0 175.7 jit_solution(8337357139573605575)
XLA Ops:
  7.2 0.0 copy-start
  7.2 0.0 reduce-scatter.2.cloned.1.call-start
  7.2 0.9 fusion.21
  8.1 0.7 broadcast_add_fusion.1
  8.8 0.7 iota_compare_fusion.1
  9.5 0.1 add.75
  9.6 0.7 broadcast_add_fusion
  10.3 1.3 select_select_fusion
  11.6 0.6 fusion.5
  12.3 0.1 fusion.23
  12.4 0.0 copy-start.3
  12.4 0.5 convolution_convert_fusion.1
  12.9 1.1 copy.40
  14.0 25.6 %all_to_all.34 = bf16[8,2,64,512]{3,1,0,2:T(2,128)(2,1)S(1)} all-to-all(bf16[8,2,64,512]{3,1,0,2:T(2,128)(2,1)S(1)} %copy.40), channel_id=1, replica_groups=mesh['dp'=32,'rep'=8] {'dp'}, dimensions={2} | all-to-all | bytes 2097152 | tf_op jit(solution)/shard_map/all_to_all | solution.py:68
  39.6 0.4 fusion.2
  40.0 0.3 copy.42
  40.3 5.1 %convolution_convert_fusion = bf16[512,7168]{1,0:T(8,128)(2,1)} fusion(bf16[256,7168]{1,0:T(8,128)(2,1)S(1)} %copy-done.2, bf16[64,8,2,128]{3,2,1,0:T(2,128)(2,1)S(1)} %bitcast.53), kind=kOutput, calls=%fused_computation.8 | convolution fusion | flops 1882718208 | bytes 11272192 | tf_op jit(solution)/shard_map/dot_general | solution.py:74
  45.4 0.0 reduce-scatter.2.cloned.1.call-update
  45.4 0.6 copy-done.4
  46.0 0.0 copy-done.5
  46.0 0.1 select_reduce_fusion.1
  46.1 0.7 gather_fusion.2
  46.8 0.1 fusion.13
  46.9 0.7 copy.37
  47.6 4.0 %all-to-all-start.1 = ((s32[32,1,1]{2,1,0:T(1,128)}), s32[32,1,1]{2,1,0:T(1,128)S(1)}, u32[]{:S(2)}, u32[]{:S(2)}) async-start(s32[32,1,1]{2,1,0:T(1,128)} %copy.37), calls=%async_computation.1 | async-start | bytes 32768 | tf_op jit(solution)/shard_map/all_to_all | solution.py:89
  51.6 2.3 %gather_fusion.1 = bf16[32,64,576]{2,1,0:T(8,128)(2,1)} fusion(bf16[8,64,576]{2,1,0:T(8,128)(2,1)S(1)} %select_select_fusion, s32[1024]{0:T(1024)S(1)} %pad_clamp_fusion.1), kind=kCustom, calls=%fused_computation.1 | custom fusion | bytes 4718720 | tf_op jit(solution)/shard_map/gather | solution.py:19
  53.9 0.1 fusion.14
  54.0 3.5 %broadcast_select_fusion = bf16[32,64,576]{2,1,0:T(8,128)(2,1)} fusion(bf16[32,64,576]{2,1,0:T(8,128)(2,1)} %gather_fusion.1, pred[32]{0:T(512)(128)(4,1)S(1)} %fusion.13), kind=kLoop, calls=%fused_computation.9 | loop fusion | flops 1179648 | bytes 4718624 | tf_op jit(solution)/shard_map/jit(_where)/select_n | solution.py:21
  57.6 0.2 reduce-window.16
  57.7 0.7 all-to-all-done.1
  58.5 6.7 %all-to-all-start = ((bf16[32,64,576]{2,1,0:T(8,128)(2,1)}), bf16[32,64,576]{2,1,0:T(8,128)(2,1)}, u32[]{:S(2)}, u32[]{:S(2)}) async-start(bf16[32,64,576]{2,1,0:T(8,128)(2,1)} %broadcast_select_fusion), calls=%async_computation | async-start | bytes 5242880 | tf_op jit(solution)/shard_map/all_to_all | solution.py:88
  65.2 0.1 select_reduce_fusion.2
  65.3 0.6 gather_fusion
  65.9 73.2 %reduce-scatter.2.cloned.1.call-done = bf16[16,7168]{1,0:T(8,128)(2,1)} async-done(((bf16[512,7168]{1,0:T(8,128)(2,1)}), bf16[16,7168]{1,0:T(8,128)(2,1)}) %reduce-scatter.2.cloned.1.call-update) | async-done | bytes 229392 | tf_op jit(solution)/shard_map/reduce_scatter | solution.py:73
  139.1 1.0 reshape.236
  140.1 2.4 %gather_fusion.5 = bf16[32,2,7168]{2,1,0:T(2,128)(2,1)S(1)} fusion(bf16[8,2,7168]{2,1,0:T(2,128)(2,1)S(1)} %reshape.236, s32[1024]{0:T(1024)S(1)} %pad_clamp_fusion.1), kind=kCustom, calls=%fused_computation.5 | custom fusion | bytes 1835136 | tf_op jit(solution)/shard_map/gather | solution.py:19
  142.5 1.8 %broadcast_select_fusion.1 = bf16[32,2,7168]{2,1,0:T(2,128)(2,1)} fusion(bf16[32,2,7168]{2,1,0:T(2,128)(2,1)S(1)} %gather_fusion.5, pred[32]{0:T(512)(128)(4,1)S(1)} %fusion.13), kind=kLoop, calls=%fused_computation.10 | loop fusion | flops 458752 | bytes 1835040 | tf_op jit(solution)/shard_map/jit(_where)/select_n | solution.py:21
  144.3 7.4 %all-to-all-start.3 = ((bf16[32,2,7168]{2,1,0:T(2,128)(2,1)}), bf16[32,2,7168]{2,1,0:T(2,128)(2,1)S(1)}, u32[]{:S(2)}, u32[]{:S(2)}) async-start(bf16[32,2,7168]{2,1,0:T(2,128)(2,1)} %broadcast_select_fusion.1), calls=%async_computation.4 | async-start | bytes 1835008 | tf_op jit(solution)/shard_map/all_to_all | solution.py:90
  151.7 0.7 compare_reduce_fusion
  152.3 0.1 reduce-window.17
  152.4 0.1 add_reduce_fusion
  152.5 0.1 select_reduce_fusion
  152.6 2.3 %gather_fusion.3 = bf16[4,64,576]{2,1,0:T(8,128)(2,1)S(1)} fusion(bf16[32,64,576]{2,1,0:T(8,128)(2,1)} %all-to-all-done, s32[1024]{0:T(1024)S(1)} %pad_clamp_fusion), kind=kCustom, calls=%fused_computation.3 | custom fusion | bytes 589840 | tf_op jit(solution)/shard_map/gather | solution.py:31
  155.0 0.9 pad_maximum_fusion
  155.9 0.8 gather_fusion.4
  156.7 10.4 %all-to-all-done.3 = bf16[32,2,7168]{2,1,0:T(2,128)(2,1)S(1)} async-done(((bf16[32,2,7168]{2,1,0:T(2,128)(2,1)}), bf16[32,2,7168]{2,1,0:T(2,128)(2,1)S(1)}, u32[]{:S(2)}, u32[]{:S(2)}) %all-to-all-start.3) | async-done | bytes 917536 | tf_op jit(solution)/shard_map/all_to_all | solution.py:90
  167.1 0.8 gather_fusion.6
  167.9 1.0 pad_maximum_fusion.1
  (20 shorter events, 0.1 us)
Async XLA Ops:
  7.2 4.5 %copy-start = (bf16[8,2,64,576]{3,2,1,0:T(8,128)(2,1)S(1)}, bf16[8,2,64,576]{3,2,1,0:T(8,128)(2,1)}, u32[]{:S(2)}) copy-start(bf16[8,2,64,576]{3,2,1,0:T(8,128)(2,1)} %param.10) | copy-start | bytes 3538948
  7.2 131.9 %reduce-scatter.2.cloned.1.call-start = ((), (), s32[]{:S(2)}) async-start(), calls=%async_computation.5 | async-start | bytes 7569408 | tf_op jit(solution)/shard_map/reduce_scatter | solution.py:73
  12.4 27.2 %copy-start.3 = (bf16[2,512,128]{2,1,0:T(8,128)(2,1)S(1)}, bf16[2,512,128]{2,1,0:T(8,128)(2,1)}, u32[]{:S(2)}) copy-start(bf16[2,512,128]{2,1,0:T(8,128)(2,1)} %param.12) | copy-start | bytes 786436
  14.0 26.3 %copy-start.2 = (bf16[256,7168]{1,0:T(8,128)(2,1)S(1)}, bf16[256,7168]{1,0:T(8,128)(2,1)}, u32[]{:S(2)}) copy-start(bf16[256,7168]{1,0:T(8,128)(2,1)} %param.13) | copy-start | bytes 11010052
  45.4 0.7 copy-start.4
  45.4 0.7 copy-start.5
  45.4 0.8 copy-start.1
  47.6 10.8 %all-to-all-start.1 = ((s32[32,1,1]{2,1,0:T(1,128)}), s32[32,1,1]{2,1,0:T(1,128)S(1)}, u32[]{:S(2)}, u32[]{:S(2)}) async-start(s32[32,1,1]{2,1,0:T(1,128)} %copy.37), calls=%async_computation.1 | async-start | bytes 32768 | tf_op jit(solution)/shard_map/all_to_all | solution.py:89
  58.5 85.8 %all-to-all-start = ((bf16[32,64,576]{2,1,0:T(8,128)(2,1)}), bf16[32,64,576]{2,1,0:T(8,128)(2,1)}, u32[]{:S(2)}, u32[]{:S(2)}) async-start(bf16[32,64,576]{2,1,0:T(8,128)(2,1)} %broadcast_select_fusion), calls=%async_computation | async-start | bytes 5242880 | tf_op jit(solution)/shard_map/all_to_all | solution.py:88
  144.3 22.8 %all-to-all-start.3 = ((bf16[32,2,7168]{2,1,0:T(2,128)(2,1)}), bf16[32,2,7168]{2,1,0:T(2,128)(2,1)S(1)}, u32[]{:S(2)}, u32[]{:S(2)}) async-start(bf16[32,2,7168]{2,1,0:T(2,128)(2,1)} %broadcast_select_fusion.1), calls=%async_computation.4 | async-start | bytes 1835008 | tf_op jit(solution)/shard_map/all_to_all | solution.py:90
Sparse Core Ops, SparseCore 0:
  45.5 93.5 reduce-scatter.1
where the time goes:
time: 176 us
  waiting for transfers between devices  84.3 us (48%)
  blocking collectives  25.6 us (15%)
  starting transfers between devices  18 us (10%)
  local copies, waits for them, and re-layouts  14.6 us (8%)
  between operations  14.2 us (8%)
  other arithmetic  12.3 us (7%)
  matrix products  6.65 us (4%)
    reduce_scatter x1, waiting for transfers between devices, decode(): lax.psum_scatter(jnp.dot(flat_v, w_out, preferred_element_type=jnp.float3...  73.2 us
    all_to_all x1, blocking collectives, decode(): lax.all_to_all(latent, 'dp', split_axis=2, concat_axis=0, tiled=True)  25.6 us
    all_to_all x1, waiting for transfers between devices, per_device(): lax.all_to_all(sent[2], 'dp', split_axis=0, concat_axis=0, tiled=True)  10.4 us
    all_to_all x1, starting transfers between devices, per_device(): lax.all_to_all(sent[2], 'dp', split_axis=0, concat_axis=0, tiled=True)  7.35 us
    all_to_all x1, starting transfers between devices, per_device(): lax.all_to_all(sent[0], 'dp', split_axis=0, concat_axis=0, tiled=True)  6.69 us
    gather x3, local copies, waits for them, and re-layouts, place_rows(): picked = member[source_slot]  5.41 us
    select_n x3, other arithmetic, place_rows(): placed.append(jnp.where(shaped, picked, jnp.zeros((), member.dtype)))  5.31 us
    dot_general x1, matrix products, decode(): jnp.dot(flat_v, w_out, preferred_element_type=jnp.float32)  5.06 us
  transfers between devices with their start and end apart: 4, of which 3 were waited for; matrix products, arithmetic and copies ran while one was open for 11% of the time, Pallas kernels for 0%

commit v1 on v0

v1 whole, which is shorter than its diff:
```python
import math

import jax
import jax.numpy as jnp
from jax import lax
from jax.experimental import pallas as pl
from jax.experimental.pallas import tpu as pltpu
from jax.sharding import PartitionSpec as P

D = 7168
LAT = 512
ENT = 576
VD = 128
ROPE = 64
CAP = 64
ROWS = 8
MOVE = 4
SUBS = 7
SUB = D // SUBS
HALF = SUB // 2
MESH = pl.DeviceIdType.MESH
BF = jnp.bfloat16
F32 = jnp.float32
I32 = jnp.int32


def iota(shape, dim):
    return lax.broadcasted_iota(I32, shape, dim)


def one_hot(mask):
    return jnp.where(mask, 1.0, 0.0).astype(BF)


def mm(a, b):
    return jnp.dot(a, b, preferred_element_type=F32)


def kernel(
    len_s, out_s, tgt_s, fresh_v, cache_h, q_h, wuv_h, wout_h,
    nc_h, att_h,
    upd, q_v, wuv, wout, lat, in1, in2, vals, gall,
    part, rl, mg, ac, p2, rl2, mg2, ac2, att,
    cand, sib, sel, fin, swp, outc, tabv, tabs,
    lsem, gsem, grec, wsem, wrec, s1, r1, s2, r2, sv, rv,
    srs, rrs, cs, cr, osem,
):
    dp = lax.axis_index("dp")
    x, y, c = dp // 8, (dp // 2) % 4, dp % 2
    f = x + c * (y - x)
    g = y + c * (x - y)

    def dev(ff, gg, cc):
        xx = ff + c * (gg - ff)
        yy = gg + c * (ff - gg)
        return (xx * 4 + yy) * 2 + cc

    def on_f(k):
        return {"dp": dev((f + k) % 4, g, c)}

    def on_g(k):
        return {"dp": dev(f, (g + k) % 4, c)}

    sibling = {"dp": dev(f, g, 1 - c)}

    def send(src, dst, ss, rs, device):
        copy = pltpu.make_async_remote_copy(
            src_ref=src, dst_ref=dst, send_sem=ss, recv_sem=rs, device_id=device, device_id_type=MESH
        )
        copy.start()
        return copy

    loads = [
        pltpu.make_async_copy(cache_h, upd, lsem.at[0]),
        pltpu.make_async_copy(q_h, q_v, lsem.at[1]),
        pltpu.make_async_copy(wuv_h, wuv.at[pl.ds(2 * c, 2)], lsem.at[2]),
        pltpu.make_async_copy(wout_h, wout.at[pl.ds(pl.multiple_of(256 * c, 256), 256)], lsem.at[3]),
    ]
    for load in loads:
        load.start()

    barrier = pltpu.get_barrier_semaphore()
    for k in (1, 2, 3):
        pl.semaphore_signal(barrier, inc=1, device_id=on_f(k), device_id_type=MESH)
        pl.semaphore_signal(barrier, inc=1, device_id=on_g(k), device_id_type=MESH)
    pl.semaphore_signal(barrier, inc=1, device_id=sibling, device_id_type=MESH)

    lane = iota((1, 128), 1)
    slot_lane = (lane >> 1) & 7
    dest_row = jnp.full((1, 128), -1.0, F32)
    target_row = jnp.zeros((1, 128), F32)
    for m in range(MOVE):
        goal = tgt_s[m].astype(F32)
        dest_row = jnp.where(slot_lane == out_s[m], goal, dest_row)
        target_row = jnp.where((lane & 3) == m, goal, target_row)
    row_of = iota((8, 128), 0)
    gall[c, 0, 0] = jnp.where(row_of == 0, dest_row, target_row)

    pl.semaphore_wait(barrier, 7)

    g1 = [send(gall.at[c, 0, 0], gall.at[c, 0, k], gsem.at[k - 1], grec.at[k - 1], on_f(k)) for k in (1, 2, 3)]

    loads[0].wait()
    slot = iota((CAP, 1), 0)
    for r in range(ROWS):
        fresh = fresh_v[r].astype(F32)
        old = upd[r].astype(F32)
        new = jnp.where(slot == len_s[r], fresh[0:1], old)
        new = jnp.where(slot == len_s[r] + 1, fresh[1:2], new)
        upd[r] = new.astype(BF)
    mine = pl.multiple_of(c * 32, 32)
    theirs = pl.multiple_of((1 - c) * 32, 32)
    for m in range(MOVE):
        sib[m] = upd[out_s[m], pl.ds(theirs, 32)]
        cand[0, c, m] = upd[out_s[m], pl.ds(mine, 32)]
    c0 = send(sib, cand.at[0, c], cs.at[0], cr.at[0], sibling)
    w0 = send(wuv_h, wuv.at[pl.ds(2 * c, 2)], wsem.at[0], wrec.at[0], sibling)
    w1 = send(wout_h, wout.at[pl.ds(pl.multiple_of(256 * c, 256), 256)], wsem.at[1], wrec.at[1], sibling)

    ro = iota((512, 1), 0)
    of, og, oh, orow, ostep = ro >> 7, (ro >> 5) & 3, (ro >> 3) & 3, (ro >> 1) & 3, ro & 1
    ox = of + c * (og - of)
    oy = og + c * (of - og)
    wanted = orow * 128 + ostep * 64 + (ox * 4 + oy) * 4 + oh
    turn = one_hot(iota((512, 512), 1) == wanted)
    qi = iota((512, 256), 0)
    ki = iota((512, 256), 1)
    same_row = (qi >> 7) == (ki >> 6)
    ahead = (ki & 63) - ((qi >> 6) & 1)
    klane = iota((1, 256), 1) >> 6
    scale = 1.0 / math.sqrt(VD + ROPE)

    loads[1].wait()
    l1 = {}
    for grp in range(2):
        queries = q_v[4 * grp : 4 * grp + 4].reshape(512, ENT)
        keys = upd[4 * grp : 4 * grp + 4].reshape(256, ENT)
        scores = lax.dot_general(queries, keys, (((1,), (1,)), ((), ())), preferred_element_type=F32) * scale
        limit = jnp.zeros((1, 256), I32)
        for r in range(4):
            limit = jnp.where(klane == r, len_s[4 * grp + r], limit)
        scores = jnp.where(same_row & (ahead <= limit), scores, -1e30)
        weights = jnp.exp(scores - jnp.max(scores, axis=1, keepdims=True))
        probs = (weights / jnp.sum(weights, axis=1, keepdims=True)).astype(BF)
        turned = mm(turn, probs).astype(BF)
        latent = mm(turned, keys[:, :LAT]).astype(BF)
        lat[grp] = latent.reshape(4, 4, 32, LAT)
        for k in (1, 2, 3):
            l1[grp, k] = send(lat.at[grp, (f + k) % 4], in1.at[grp, k], s1.at[grp, k - 1], r1.at[grp, k - 1], on_f(k))

    for copy in g1:
        copy.wait_recv()
    g2 = [send(gall.at[c, 0], gall.at[c, k], gsem.at[2 + k], grec.at[2 + k], on_g(k)) for k in (1, 2, 3)]
    c0.wait_recv()
    c1 = [send(cand.at[0], cand.at[k], cs.at[k], cr.at[k], on_f(k)) for k in (1, 2, 3)]

    l2 = {}
    for grp in range(2):
        for k in range(4):
            if k:
                l1[grp, k].wait_recv()
                block = in1.at[grp, k]
            else:
                block = lat.at[grp, f]
            for j in (1, 2, 3):
                l2[grp, k, j] = send(
                    block.at[(g + j) % 4], in2.at[j, k, grp], s2.at[grp, k, j - 1], r2.at[grp, k, j - 1], on_g(j)
                )
            if k:
                in2[0, k, grp] = in1[grp, k, g]
            else:
                in2[0, k, grp] = lat[grp, f, g]

    for copy in g2:
        copy.wait_recv()
    g3 = send(gall.at[c], gall.at[c], gsem.at[6], grec.at[6], sibling)

    def source(l):
        cs_, dg_, df_ = l >> 8, (l >> 6) & 3, (l >> 4) & 3
        fs = (x + cs_ * (y - x) - df_) & 3
        gs = (y + cs_ * (x - y) - dg_) & 3
        return ((fs + cs_ * (gs - fs)) * 4 + gs + cs_ * (fs - gs)) * 2 + cs_

    wide = iota((1, 512), 1)
    tall = iota((512, 1), 0)
    from_w, from_t = source(wide), source(tall)
    slot_w, slot_t = (wide >> 1) & 7, (tall >> 1) & 7
    even = (tall & 1) == 0
    before = one_hot(even & (from_t < from_w))
    within = one_hot(even & (from_t == from_w) & (slot_t < slot_w))
    nr = iota((256, 1), 0)
    nf, ng = nr >> 6, (nr >> 4) & 3
    ndev = ((nf + c * (ng - nf)) * 4 + ng + c * (nf - ng)) * 2 + c
    nslot, nstep = (nr >> 1) & 7, nr & 1

    g3.wait_recv()
    rows = gall[...].reshape(32, 8, 128)
    sub8 = iota((8, 128), 0)
    lane8 = iota((8, 128), 1) >> 4
    pieces = []
    for v in range(4):
        total = jnp.zeros((1, 128), F32)
        for b in range(8):
            total = total + jnp.where((lane >> 4) == b, rows[8 * v + b][0:1], 0.0)
        pieces.append(total)
    dest_w = jnp.concatenate(pieces, axis=1).astype(I32)
    comes = dest_w == ndev
    stays = (dest_w < 0) & (from_w == ndev)
    rank_in = mm(one_hot(comes), before)
    rank_stay = mm(one_hot(stays), within)
    place = jnp.where(comes, rank_in + 4.0, jnp.where(stays, rank_stay, -1.0))
    order = one_hot((place == nslot.astype(F32)) & ((wide & 1) == nstep))

    table = jnp.zeros((1, 128), F32)
    l_dg, l_df, l_sc = lane >> 5, (lane >> 3) & 3, (lane >> 2) & 1
    for sc in range(2):
        for a in range(4):
            for b in range(4):
                row = rows[sc * 16 + a * 4 + b][1:2]
                swapped = sc + c - 2 * sc * c
                la = a + swapped * (b - a)
                lb = b + swapped * (a - b)
                table = table + jnp.where((l_sc == sc) & (l_dg == la) & (l_df == lb), row, 0.0)
    table = table.astype(I32)
    lt, lw = iota((128, 128), 0), iota((128, 128), 1)
    earlier = one_hot(((lt >> 5) == (lw >> 5)) & (lt < lw))

    def mover(l):
        fs = (f - ((l >> 3) & 3)) & 3
        gs = (g - (l >> 5)) & 3
        return ((fs + c * (gs - fs)) * 4 + gs + c * (fs - gs)) * 2 + ((l >> 2) & 1)

    lower = one_hot(mover(iota((128, 1), 0)) < mover(lane))
    tr = iota((32, 128), 0)
    tdg, tcore, tk = tr >> 3, (tr >> 2) & 1, tr & 3
    tl = iota((32, 128), 1)
    tg = (g + tdg) & 3
    tdev = ((f + c * (tg - f)) * 4 + tg + c * (f - tg)) * 2 + tcore
    hit = (table == tdev) & (tl < 32)
    nth = mm(one_hot(hit), earlier)
    pick = jnp.sum(jnp.where(hit & (nth == tk.astype(F32)), tl, 0), axis=1, keepdims=True)
    ur = iota((8, 128), 0)
    ucore, uj = ur >> 2, ur & 3
    udev = ((f + c * (g - f)) * 4 + g + c * (f - g)) * 2 + ucore
    own = table == udev
    spot = (lane >> 5) * 8 + ucore * 4 + mm(one_hot(own), earlier).astype(I32)
    turn_in = mm(one_hot(own), lower)
    last = jnp.sum(jnp.where(own & (turn_in == uj.astype(F32)), spot, 0), axis=1, keepdims=True)
    tabv[0:32] = jnp.broadcast_to(pick, (32, 128))
    tabv[32:40] = jnp.broadcast_to(last, (8, 128))
    tcopy = pltpu.make_async_copy(tabv, tabs, lsem.at[4])
    tcopy.start()
    tcopy.wait()

    for copy in c1:
        copy.wait_recv()
    c2 = []
    for j in (1, 2, 3, 0):
        for i in range(8):
            which = tabs[j * 8 + i, 0]
            chosen = cand[which >> 3, (which >> 2) & 1, which & 3]
            if j:
                sel[j - 1, i] = chosen
            else:
                fin[0, i] = chosen
        if j:
            c2.append(send(sel.at[j - 1], fin.at[j], cs.at[3 + j], cr.at[3 + j], on_g(j)))

    loads[2].wait()
    w0.wait_recv()
    swaps = []
    for j in range(4):
        if j:
            for grp in range(2):
                for k in range(4):
                    l2[grp, k, j].wait_recv()
        block = in2[j].reshape(256, LAT)
        for h in range(4):
            value = mm(block, wuv[h]).reshape(8, 4, 8, VD)[:, h].reshape(64, VD)
            vals[c, pl.ds(64 * j, 64), pl.ds(VD * h, VD)] = value.astype(BF)
        swaps.append(
            send(vals.at[c, pl.ds(64 * j, 64)], vals.at[c, pl.ds(64 * j, 64)], sv.at[j], rv.at[j], sibling)
        )
    for copy in swaps:
        copy.wait_recv()
    flat = mm(order, vals[...].reshape(512, 512)).astype(BF)
    loads[3].wait()
    w1.wait_recv()

    f1, f2, f3 = (f + 1) % 4, (f + 2) % 4, (f + 3) % 4
    h1, h2, h3 = (g + 1) % 4, (g + 2) % 4, (g + 3) % 4
    low, high = pl.ds(0, 32), pl.ds(32, 32)
    left, right = pl.ds(0, HALF), pl.ds(HALF, HALF)

    def rs(s, i, src, dst, device):
        return pltpu.make_async_remote_copy(
            src_ref=src, dst_ref=dst, send_sem=srs.at[s, i], recv_sem=rrs.at[s, i],
            device_id=device, device_id_type=MESH,
        )

    def copy_of(s, i):
        table = (
            lambda: rs(s, 0, part.at[s, f2, low], rl.at[s, 0], on_f(1)),
            lambda: rs(s, 1, part.at[s, f2, high], rl.at[s, 1], on_f(3)),
            lambda: rs(s, 2, part.at[s, f1, high], ac.at[s, 0, high], on_f(1)),
            lambda: rs(s, 3, part.at[s, f3, low], ac.at[s, 1, low], on_f(3)),
            lambda: rs(s, 4, mg.at[s, 0], ac.at[s, 0, low], on_f(1)),
            lambda: rs(s, 5, mg.at[s, 1], ac.at[s, 1, high], on_f(3)),
            lambda: rs(s, 6, p2.at[s, h2, :, left], rl2.at[s, 0], on_g(1)),
            lambda: rs(s, 7, p2.at[s, h2, :, right], rl2.at[s, 1], on_g(3)),
            lambda: rs(s, 8, p2.at[s, h1, :, right], ac2.at[s, 0, :, right], on_g(1)),
            lambda: rs(s, 9, p2.at[s, h3, :, left], ac2.at[s, 1, :, left], on_g(3)),
            lambda: rs(s, 10, mg2.at[s, 0], ac2.at[s, 0, :, left], on_g(1)),
            lambda: rs(s, 11, mg2.at[s, 1], ac2.at[s, 1, :, right], on_g(3)),
        )
        return table[i]()

    def step(t, carry):
        @pl.when(t < SUBS)
        def _():
            s = t
            cols = pl.ds(pl.multiple_of(s * SUB, SUB), SUB)
            part[s] = mm(flat, wout[:, cols]).astype(BF).reshape(4, 64, SUB)
            for i in range(4):
                copy_of(s, i).start()

        @pl.when((t >= 1) & (t < SUBS + 1))
        def _():
            s = t - 1
            copy_of(s, 0).wait_recv()
            mg[s, 0] = (part[s, f1, low].astype(F32) + rl[s, 0].astype(F32)).astype(BF)
            copy_of(s, 4).start()
            copy_of(s, 1).wait_recv()
            mg[s, 1] = (part[s, f3, high].astype(F32) + rl[s, 1].astype(F32)).astype(BF)
            copy_of(s, 5).start()

        @pl.when((t >= 2) & (t < SUBS + 2))
        def _():
            s = t - 2
            for i in (2, 3, 4, 5):
                copy_of(s, i).wait_recv()
            whole = part[s, f].astype(F32) + ac[s, 0].astype(F32) + ac[s, 1].astype(F32)
            p2[s] = whole.astype(BF).reshape(4, 16, SUB)
            for i in (6, 7, 8, 9):
                copy_of(s, i).start()

        @pl.when((t >= 3) & (t < SUBS + 3))
        def _():
            s = t - 3
            copy_of(s, 6).wait_recv()
            mg2[s, 0] = (p2[s, h1, :, left].astype(F32) + rl2[s, 0].astype(F32)).astype(BF)
            copy_of(s, 10).start()
            copy_of(s, 7).wait_recv()
            mg2[s, 1] = (p2[s, h3, :, right].astype(F32) + rl2[s, 1].astype(F32)).astype(BF)
            copy_of(s, 11).start()

        @pl.when(t >= 4)
        def _():
            s = t - 4
            for i in (8, 9, 10, 11):
                copy_of(s, i).wait_recv()
            whole = p2[s, g].astype(F32) + ac2[s, 0].astype(F32) + ac2[s, 1].astype(F32)
            att[s] = whole.astype(BF)
            cols = pl.ds(pl.multiple_of(s * SUB, SUB), SUB)
            pltpu.make_async_copy(att.at[s], att_h.at[:, cols], osem.at[s]).start()

        return carry

    lax.fori_loop(0, SUBS + 4, step, 0)

    for copy in c2:
        copy.wait_recv()
    for j in range(MOVE):
        there = tabs[32 + (1 - c) * 4 + j, 0]
        here = tabs[32 + c * 4 + j, 0]
        swp[j] = fin[there >> 3, there & 7]
        outc[MOVE + j, pl.ds(mine, 32)] = fin[here >> 3, here & 7]
    c3 = send(swp, outc.at[pl.ds(MOVE, MOVE), pl.ds(mine, 32)], cs.at[7], cr.at[7], sibling)
    kept = [0] * MOVE
    count = 0
    for r in range(ROWS):
        gone = (out_s[0] == r) | (out_s[1] == r) | (out_s[2] == r) | (out_s[3] == r)
        stay = 1 - gone.astype(I32)
        for j in range(MOVE):
            kept[j] = kept[j] + jnp.where(count == j, stay * r, 0)
        count = count + stay
    for j in range(MOVE):
        outc[j] = upd[kept[j]]
    c3.wait_recv()
    finish = pltpu.make_async_copy(outc, nc_h, lsem.at[5])
    finish.start()

    for copy in g1 + g2 + [g3, c0, w0, w1] + c1 + c2 + swaps + [c3]:
        copy.wait_send()
    for copy in list(l1.values()) + list(l2.values()):
        copy.wait_send()

    def drain(s, carry):
        for i in range(12):
            copy_of(s, i).wait_send()
        cols = pl.ds(pl.multiple_of(s * SUB, SUB), SUB)
        pltpu.make_async_copy(att.at[s], att_h.at[:, cols], osem.at[s]).wait()
        return carry

    lax.fori_loop(0, SUBS, drain, 0)
    finish.wait()


def per_device(cache, lengths, queries, fresh, w_uv, w_out, outgoing, targets):
    smem = pl.BlockSpec(memory_space=pltpu.SMEM)
    hbm = pl.BlockSpec(memory_space=pl.ANY)
    dma = pltpu.SemaphoreType.DMA
    scratch = [
        pltpu.VMEM((ROWS, CAP, ENT), BF),
        pltpu.VMEM((ROWS, 128, ENT), BF),
        pltpu.VMEM((4, LAT, VD), BF),
        pltpu.VMEM((512, D), BF),
        pltpu.VMEM((2, 4, 4, 32, LAT), BF),
        pltpu.VMEM((2, 4, 4, 32, LAT), BF),
        pltpu.VMEM((4, 4, 2, 32, LAT), BF),
        pltpu.VMEM((2, 256, 512), BF),
        pltpu.VMEM((2, 4, 4, 8, 128), F32),
        pltpu.VMEM((SUBS, 4, 64, SUB), BF),
        pltpu.VMEM((SUBS, 2, 32, SUB), BF),
        pltpu.VMEM((SUBS, 2, 32, SUB), BF),
        pltpu.VMEM((SUBS, 2, 64, SUB), BF),
        pltpu.VMEM((SUBS, 4, 16, SUB), BF),
        pltpu.VMEM((SUBS, 2, 16, HALF), BF),
        pltpu.VMEM((SUBS, 2, 16, HALF), BF),
        pltpu.VMEM((SUBS, 2, 16, SUB), BF),
        pltpu.VMEM((SUBS, 16, SUB), BF),
        pltpu.VMEM((4, 2, MOVE, 32, ENT), BF),
        pltpu.VMEM((MOVE, 32, ENT), BF),
        pltpu.VMEM((3, 8, 32, ENT), BF),
        pltpu.VMEM((4, 8, 32, ENT), BF),
        pltpu.VMEM((MOVE, 32, ENT), BF),
        pltpu.VMEM((ROWS, CAP, ENT), BF),
        pltpu.VMEM((40, 128), I32),
        pltpu.SMEM((40, 128), I32),
        dma((6,)),
        dma((7,)), dma((7,)),
        dma((2,)), dma((2,)),
        dma((2, 3)), dma((2, 3)),
        dma((2, 4, 3)), dma((2, 4, 3)),
        dma((4,)), dma((4,)),
        dma((SUBS, 12)), dma((SUBS, 12)),
        dma((8,)), dma((8,)),
        dma((SUBS,)),
    ]
    new_cache, attended = pl.pallas_call(
        kernel,
        out_shape=(
            jax.ShapeDtypeStruct((ROWS, CAP, ENT), BF),
            jax.ShapeDtypeStruct((2 * ROWS, D), BF),
        ),
        in_specs=[smem, smem, smem, pl.BlockSpec(memory_space=pltpu.VMEM), hbm, hbm, hbm, hbm],
        out_specs=(hbm, hbm),
        scratch_shapes=scratch,
        compiler_params=pltpu.CompilerParams(
            collective_id=0, has_side_effects=True, vmem_limit_bytes=48 * 1024 * 1024
        ),
        cost_estimate=pl.CostEstimate(flops=4 * 10**9, bytes_accessed=8 * 10**6, transcendentals=10**6),
        name="mla_decode",
    )(lengths, outgoing, targets, fresh, cache, queries.reshape(ROWS, 128, ENT), w_uv, w_out)
    return new_cache, attended.reshape(ROWS, 2, D)


def solution(mesh):
    in_specs = (
        P(("rep", "dp"), None, None),
        P(("rep", "dp")),
        P(("rep", "dp"), None, None, None),
        P(("rep", "dp"), None, None),
        P("dp", None, None),
        P("dp", None),
        P(("rep", "dp")),
        P(("rep", "dp")),
    )
    out_specs = (P(("rep", "dp"), None, None), P(("rep", "dp"), None, None))
    return jax.shard_map(
        per_device, mesh=mesh, in_specs=in_specs, out_specs=out_specs, check_vma=False
    )
```

time: 176 us -> 78.6 us (0.45)
  waiting for transfers between devices: 84.3 us -> 0 us
  Pallas kernels: 0 us -> 70 us
  blocking collectives: 25.6 us -> 0 us
  starting transfers between devices: 18 us -> 0 us
  between operations: 14.2 us -> 0.66 us
  other arithmetic: 12.3 us -> 0 us
  local copies, waits for them, and re-layouts: 14.6 us -> 7.65 us
  matrix products: 6.65 us -> 0 us
    reduce_scatter x1 -> x0, waiting for transfers between devices: 73.2 us -> none  [decode(): lax.psum_scatter(jnp.dot(flat_v, w_out, preferred_element_type=jnp.float3...]
    pallas_call x0 -> x1, Pallas kernels: none -> 70 us  [per_device(): pl.pallas_call(kernel, out_shape=(jax.ShapeDtypeStruct((ROWS, CAP, ENT),...]
    all_to_all x1 -> x0, blocking collectives: 25.6 us -> none  [decode(): lax.all_to_all(latent, 'dp', split_axis=2, concat_axis=0, tiled=True)]
    all_to_all x3 -> x0, starting transfers between devices: 18 us -> none  [the longest x1 7.35 us: per_device(): lax.all_to_all(sent[2], 'dp', split_axis=0, concat_axis=0, tiled=True)]
    all_to_all x3 -> x0, waiting for transfers between devices: 11.1 us -> none  [the longest x1 10.4 us: per_device(): lax.all_to_all(sent[2], 'dp', split_axis=0, concat_axis=0, tiled=True)]
    gather x7 -> x0, local copies, waits for them, and re-layouts: 9.92 us -> none  [the longest x3 5.41 us: place_rows(): picked = member[source_slot]]
    select_n x7 -> x0, other arithmetic: 6.65 us -> none  [the longest x3 5.31 us: place_rows(): placed.append(jnp.where(shaped, picked, jnp.zeros((), member.dtype)))]
    dot_general x4 -> x0, matrix products: 6.65 us -> none  [the longest x1 5.06 us: decode(): jnp.dot(flat_v, w_out, preferred_element_type=jnp.float32)]
  transfers between devices with their start and end apart: 4 -> 0, of which waited for: 3 -> 0; matrix products, arithmetic and copies ran while one was open for 11% -> 0% of each run, Pallas kernels for 0% -> 0%
where the time goes in v1:
time: 78.6 us; the launch traced here: 78.3 us
  Pallas kernels  70 us (89%)
  local copies, waits for them, and re-layouts  7.65 us (10%)
    pallas_call x1, Pallas kernels, per_device(): pl.pallas_call(kernel, out_shape=(jax.ShapeDtypeStruct((ROWS, CAP, ENT),...  70 us
    unnamed x15, local copies, waits for them, and re-layouts  6.87 us

profile of v1, /device:TPU:1, one launch (start us, length us, event | category | flops | bytes accessed | tf_op | source)
XLA Modules:
  0.0 78.3 jit_solution(9797674100378291469)
XLA Ops:
  0.6 0.0 copy-start
  0.6 1.3 %copy-done = bf16[8,2,64,576]{3,2,1,0:T(8,128)(2,1)S(1)} copy-done((bf16[8,2,64,576]{3,2,1,0:T(8,128)(2,1)S(1)}, bf16[8,2,64,576]{3,2,1,0:T(8,128)(2,1)}, u32[]{:S(2)}) %copy-start) | copy-done | bytes 1179672
  1.9 0.0 copy-start.1
  2.0 1.1 %copy-done.1 = bf16[8,64,576]{2,1,0:T(8,128)(2,1)S(1)} copy-done((bf16[8,64,576]{2,1,0:T(8,128)(2,1)S(1)}, bf16[8,64,576]{2,1,0:T(8,128)(2,1)}, u32[]{:S(2)}) %copy-start.1) | copy-done | bytes 589848
  3.0 0.0 copy-start.2
  3.0 0.9 %copy-done.2 = bf16[2,512,128]{2,1,0:T(8,128)(2,1)S(1)} copy-done((bf16[2,512,128]{2,1,0:T(8,128)(2,1)S(1)}, bf16[2,512,128]{2,1,0:T(8,128)(2,1)}, u32[]{:S(2)}) %copy-start.2) | copy-done | bytes 262168
  4.0 0.0 copy-start.3
  4.0 0.7 copy-done.3
  4.7 0.0 copy-start.4
  4.7 0.7 copy-done.4
  5.4 0.0 copy-start.5
  5.4 0.7 copy-done.5
  6.0 0.0 copy-start.6
  6.0 0.7 copy-done.6
  6.7 70.0 %mla_decode.1 = (bf16[8,64,576]{2,1,0:T(8,128)(2,1)S(1)}, bf16[16,7168]{1,0:T(8,128)(2,1)S(1)}) custom-call(s32[8]{0:T(128)S(1)} %copy-done.4, s32[4]{0:T(128)S(1)} %copy-done.5, s32[4]{0:T(128)S(1)} %copy-done.6, bf16[8,2,576]{2,1,0:T(2,128)(2,1)S(1)} %copy-done.3, bf16[8,64,576]{2,1,0:T(8,128)(2,1)S(1)} %copy-done.1, bf16[8,128,576]{2,1,0:T(8,128)(2,1)S(1)} %bitcast.1, ...), custom_call_target="tpu_custom_call" | custom-call | flops 4000000000 | bytes 8000000 | tf_op jit(solution)/shard_map/mla_decode/pallas_call | solution.py:450
  76.7 0.8 reshape.11
  77.5 0.8 %copy.11 = bf16[8,64,576]{2,1,0:T(8,128)(2,1)} copy(bf16[8,64,576]{2,1,0:T(8,128)(2,1)S(1)} %get-tuple-element.8) | data formatting | bytes 1179648
Async XLA Ops:
  0.6 1.3 %copy-start = (bf16[8,2,64,576]{3,2,1,0:T(8,128)(2,1)S(1)}, bf16[8,2,64,576]{3,2,1,0:T(8,128)(2,1)}, u32[]{:S(2)}) copy-start(bf16[8,2,64,576]{3,2,1,0:T(8,128)(2,1)} %param.10) | copy-start | bytes 3538948
  1.9 1.1 %copy-start.1 = (bf16[8,64,576]{2,1,0:T(8,128)(2,1)S(1)}, bf16[8,64,576]{2,1,0:T(8,128)(2,1)}, u32[]{:S(2)}) copy-start(bf16[8,64,576]{2,1,0:T(8,128)(2,1)} %cache_h.1) | copy-start | bytes 1769476
  3.0 0.9 %copy-start.2 = (bf16[2,512,128]{2,1,0:T(8,128)(2,1)S(1)}, bf16[2,512,128]{2,1,0:T(8,128)(2,1)}, u32[]{:S(2)}) copy-start(bf16[2,512,128]{2,1,0:T(8,128)(2,1)} %wuv_h.1) | copy-start | bytes 786436
  4.0 0.7 copy-start.3
  4.7 0.7 copy-start.4
  5.4 0.7 copy-start.5
  6.0 0.7 copy-start.6

commit v2 on v1

--- a/solution.py
+++ b/solution.py
@@ -37,13 +37,15 @@
 
 
 def kernel(
-    len_s, out_s, tgt_s, fresh_v, cache_h, q_h, wuv_h, wout_h,
-    nc_h, att_h,
+    len_h, out_h, tgt_h, fresh_h, cache_h, q_h, wuv_h, wout_h,
+    nc_v, att_v,
+    len_s, out_s, tgt_s, fresh_v,
+    turn, before, within, earlier, lower, order, flat,
     upd, q_v, wuv, wout, lat, in1, in2, vals, gall,
-    part, rl, mg, ac, p2, rl2, mg2, ac2, att,
-    cand, sib, sel, fin, swp, outc, tabv, tabs,
+    part, rl, mg, ac, p2, rl2, mg2, ac2,
+    cand, sib, sel, fin, swp, swr, tabv, tabs,
     lsem, gsem, grec, wsem, wrec, s1, r1, s2, r2, sv, rv,
-    srs, rrs, cs, cr, osem,
+    srs, rrs, cs, cr, cks, ckr,
 ):
     dp = lax.axis_index("dp")
     x, y, c = dp // 8, (dp // 2) % 4, dp % 2
@@ -70,13 +72,19 @@
         copy.start()
         return copy
 
+    small = [
+        pltpu.make_async_copy(out_h, out_s, lsem.at[6]),
+        pltpu.make_async_copy(tgt_h, tgt_s, lsem.at[7]),
+        pltpu.make_async_copy(len_h, len_s, lsem.at[8]),
+        pltpu.make_async_copy(fresh_h, fresh_v, lsem.at[9]),
+    ]
     loads = [
         pltpu.make_async_copy(cache_h, upd, lsem.at[0]),
         pltpu.make_async_copy(q_h, q_v, lsem.at[1]),
         pltpu.make_async_copy(wuv_h, wuv.at[pl.ds(2 * c, 2)], lsem.at[2]),
         pltpu.make_async_copy(wout_h, wout.at[pl.ds(pl.multiple_of(256 * c, 256), 256)], lsem.at[3]),
     ]
-    for load in loads:
+    for load in small + loads:
         load.start()
 
     barrier = pltpu.get_barrier_semaphore()
@@ -85,7 +93,39 @@
         pl.semaphore_signal(barrier, inc=1, device_id=on_g(k), device_id_type=MESH)
     pl.semaphore_signal(barrier, inc=1, device_id=sibling, device_id_type=MESH)
 
+    ro = iota((512, 1), 0)
+    of, og, oh, orow, ostep = ro >> 7, (ro >> 5) & 3, (ro >> 3) & 3, (ro >> 1) & 3, ro & 1
+    ox = of + c * (og - of)
+    oy = og + c * (of - og)
+    wanted = orow * 128 + ostep * 64 + (ox * 4 + oy) * 4 + oh
+    turn[...] = one_hot(iota((512, 512), 1) == wanted)
+
+    def source(l):
+        cs_, dg_, df_ = l >> 8, (l >> 6) & 3, (l >> 4) & 3
+        fs = (x + cs_ * (y - x) - df_) & 3
+        gs = (y + cs_ * (x - y) - dg_) & 3
+        return ((fs + cs_ * (gs - fs)) * 4 + gs + cs_ * (fs - gs)) * 2 + cs_
+
+    wide = iota((1, 512), 1)
+    tall = iota((512, 1), 0)
+    from_w, from_t = source(wide), source(tall)
+    slot_w, slot_t = (wide >> 1) & 7, (tall >> 1) & 7
+    even = (tall & 1) == 0
+    before[...] = one_hot(even & (from_t < from_w))
+    within[...] = one_hot(even & (from_t == from_w) & (slot_t < slot_w))
+    lt, lw = iota((128, 128), 0), iota((128, 128), 1)
     lane = iota((1, 128), 1)
+
+    def mover(l):
+        fs = (f - ((l >> 3) & 3)) & 3
+        gs = (g - (l >> 5)) & 3
+        return ((fs + c * (gs - fs)) * 4 + gs + c * (fs - gs)) * 2 + ((l >> 2) & 1)
+
+    earlier[...] = one_hot(((lt >> 5) == (lw >> 5)) & (lt < lw))
+    lower[...] = one_hot(mover(iota((128, 1), 0)) < mover(lane))
+
+    small[0].wait()
+    small[1].wait()
     slot_lane = (lane >> 1) & 7
     dest_row = jnp.full((1, 128), -1.0, F32)
     target_row = jnp.zeros((1, 128), F32)
@@ -96,11 +136,9 @@
     row_of = iota((8, 128), 0)
     gall[c, 0, 0] = jnp.where(row_of == 0, dest_row, target_row)
 
-    pl.semaphore_wait(barrier, 7)
-
-    g1 = [send(gall.at[c, 0, 0], gall.at[c, 0, k], gsem.at[k - 1], grec.at[k - 1], on_f(k)) for k in (1, 2, 3)]
-
     loads[0].wait()
+    small[2].wait()
+    small[3].wait()
     slot = iota((CAP, 1), 0)
     for r in range(ROWS):
         fresh = fresh_v[r].astype(F32)
@@ -113,16 +151,18 @@
     for m in range(MOVE):
         sib[m] = upd[out_s[m], pl.ds(theirs, 32)]
         cand[0, c, m] = upd[out_s[m], pl.ds(mine, 32)]
+
+    pl.semaphore_wait(barrier, 7)
+    g1 = [send(gall.at[c, 0, 0], gall.at[c, 0, k], gsem.at[k - 1], grec.at[k - 1], on_f(k)) for k in (1, 2, 3)]
     c0 = send(sib, cand.at[0, c], cs.at[0], cr.at[0], sibling)
+
+    def pass_rows(k, sc, src):
+        return send(src, cand.at[k, sc], cks.at[k - 1, sc], ckr.at[k - 1, sc], on_f(k if k != 2 else 1 + 2 * sc))
+
+    c1 = [pass_rows(k, c, cand.at[0, c]) for k in (1, 3)]
     w0 = send(wuv_h, wuv.at[pl.ds(2 * c, 2)], wsem.at[0], wrec.at[0], sibling)
     w1 = send(wout_h, wout.at[pl.ds(pl.multiple_of(256 * c, 256), 256)], wsem.at[1], wrec.at[1], sibling)
 
-    ro = iota((512, 1), 0)
-    of, og, oh, orow, ostep = ro >> 7, (ro >> 5) & 3, (ro >> 3) & 3, (ro >> 1) & 3, ro & 1
-    ox = of + c * (og - of)
-    oy = og + c * (of - og)
-    wanted = orow * 128 + ostep * 64 + (ox * 4 + oy) * 4 + oh
-    turn = one_hot(iota((512, 512), 1) == wanted)
     qi = iota((512, 256), 0)
     ki = iota((512, 256), 1)
     same_row = (qi >> 7) == (ki >> 6)
@@ -132,6 +172,14 @@
 
     loads[1].wait()
     l1 = {}
+    l2 = {}
+
+    def onward(grp, k, block):
+        for j in (1, 3, 2):
+            l2[grp, k, j] = send(
+                block.at[(g + j) % 4], in2.at[j, k, grp], s2.at[grp, k, j - 1], r2.at[grp, k, j - 1], on_g(j)
+            )
+
     for grp in range(2):
         queries = q_v[4 * grp : 4 * grp + 4].reshape(512, ENT)
         keys = upd[4 * grp : 4 * grp + 4].reshape(256, ENT)
@@ -142,52 +190,41 @@
         scores = jnp.where(same_row & (ahead <= limit), scores, -1e30)
         weights = jnp.exp(scores - jnp.max(scores, axis=1, keepdims=True))
         probs = (weights / jnp.sum(weights, axis=1, keepdims=True)).astype(BF)
-        turned = mm(turn, probs).astype(BF)
+        turned = mm(turn[...], probs).astype(BF)
         latent = mm(turned, keys[:, :LAT]).astype(BF)
         lat[grp] = latent.reshape(4, 4, 32, LAT)
-        for k in (1, 2, 3):
+        for k in (2, 1, 3):
             l1[grp, k] = send(lat.at[grp, (f + k) % 4], in1.at[grp, k], s1.at[grp, k - 1], r1.at[grp, k - 1], on_f(k))
-
+        onward(grp, 0, lat.at[grp, f])
+        in2[0, 0, grp] = lat[grp, f, g]
+
+    c0.wait_recv()
+    c1 += [pass_rows(k, 1 - c, cand.at[0, 1 - c]) for k in (1, 3)]
     for copy in g1:
         copy.wait_recv()
     g2 = [send(gall.at[c, 0], gall.at[c, k], gsem.at[2 + k], grec.at[2 + k], on_g(k)) for k in (1, 2, 3)]
-    c0.wait_recv()
-    c1 = [send(cand.at[0], cand.at[k], cs.at[k], cr.at[k], on_f(k)) for k in (1, 2, 3)]
-
-    l2 = {}
+
     for grp in range(2):
-        for k in range(4):
-            if k:
-                l1[grp, k].wait_recv()
-                block = in1.at[grp, k]
-            else:
-                block = lat.at[grp, f]
-            for j in (1, 2, 3):
-                l2[grp, k, j] = send(
-                    block.at[(g + j) % 4], in2.at[j, k, grp], s2.at[grp, k, j - 1], r2.at[grp, k, j - 1], on_g(j)
-                )
-            if k:
-                in2[0, k, grp] = in1[grp, k, g]
-            else:
-                in2[0, k, grp] = lat[grp, f, g]
+        for k in (1, 3, 2):
+            l1[grp, k].wait_recv()
+            onward(grp, k, in1.at[grp, k])
+            in2[0, k, grp] = in1[grp, k, g]
 
     for copy in g2:
         copy.wait_recv()
     g3 = send(gall.at[c], gall.at[c], gsem.at[6], grec.at[6], sibling)
 
-    def source(l):
-        cs_, dg_, df_ = l >> 8, (l >> 6) & 3, (l >> 4) & 3
-        fs = (x + cs_ * (y - x) - df_) & 3
-        gs = (y + cs_ * (x - y) - dg_) & 3
-        return ((fs + cs_ * (gs - fs)) * 4 + gs + cs_ * (fs - gs)) * 2 + cs_
-
-    wide = iota((1, 512), 1)
-    tall = iota((512, 1), 0)
-    from_w, from_t = source(wide), source(tall)
-    slot_w, slot_t = (wide >> 1) & 7, (tall >> 1) & 7
-    even = (tall & 1) == 0
-    before = one_hot(even & (from_t < from_w))
-    within = one_hot(even & (from_t == from_w) & (slot_t < slot_w))
+    def arrived(k, sc):
+        return pltpu.make_async_remote_copy(
+            src_ref=cand.at[0, 0], dst_ref=cand.at[k, sc], send_sem=cks.at[k - 1, sc], recv_sem=ckr.at[k - 1, sc],
+            device_id=on_f(k if k != 2 else 1 + 2 * sc), device_id_type=MESH,
+        )
+
+    arrived(1, 0).wait_recv()
+    c1.append(pass_rows(2, 0, cand.at[1, 0]))
+    arrived(3, 1).wait_recv()
+    c1.append(pass_rows(2, 1, cand.at[3, 1]))
+
     nr = iota((256, 1), 0)
     nf, ng = nr >> 6, (nr >> 4) & 3
     ndev = ((nf + c * (ng - nf)) * 4 + ng + c * (nf - ng)) * 2 + c
@@ -195,8 +232,6 @@
 
     g3.wait_recv()
     rows = gall[...].reshape(32, 8, 128)
-    sub8 = iota((8, 128), 0)
-    lane8 = iota((8, 128), 1) >> 4
     pieces = []
     for v in range(4):
         total = jnp.zeros((1, 128), F32)
@@ -206,10 +241,10 @@
     dest_w = jnp.concatenate(pieces, axis=1).astype(I32)
     comes = dest_w == ndev
     stays = (dest_w < 0) & (from_w == ndev)
-    rank_in = mm(one_hot(comes), before)
-    rank_stay = mm(one_hot(stays), within)
+    rank_in = mm(one_hot(comes), before[...])
+    rank_stay = mm(one_hot(stays), within[...])
     place = jnp.where(comes, rank_in + 4.0, jnp.where(stays, rank_stay, -1.0))
-    order = one_hot((place == nslot.astype(F32)) & ((wide & 1) == nstep))
+    order[...] = one_hot((place == nslot.astype(F32)) & ((wide & 1) == nstep))
 
     table = jnp.zeros((1, 128), F32)
     l_dg, l_df, l_sc = lane >> 5, (lane >> 3) & 3, (lane >> 2) & 1
@@ -222,54 +257,30 @@
                 lb = b + swapped * (a - b)
                 table = table + jnp.where((l_sc == sc) & (l_dg == la) & (l_df == lb), row, 0.0)
     table = table.astype(I32)
-    lt, lw = iota((128, 128), 0), iota((128, 128), 1)
-    earlier = one_hot(((lt >> 5) == (lw >> 5)) & (lt < lw))
-
-    def mover(l):
-        fs = (f - ((l >> 3) & 3)) & 3
-        gs = (g - (l >> 5)) & 3
-        return ((fs + c * (gs - fs)) * 4 + gs + c * (fs - gs)) * 2 + ((l >> 2) & 1)
-
-    lower = one_hot(mover(iota((128, 1), 0)) < mover(lane))
     tr = iota((32, 128), 0)
     tdg, tcore, tk = tr >> 3, (tr >> 2) & 1, tr & 3
     tl = iota((32, 128), 1)
     tg = (g + tdg) & 3
     tdev = ((f + c * (tg - f)) * 4 + tg + c * (f - tg)) * 2 + tcore
     hit = (table == tdev) & (tl < 32)
-    nth = mm(one_hot(hit), earlier)
+    nth = mm(one_hot(hit), earlier[...])
     pick = jnp.sum(jnp.where(hit & (nth == tk.astype(F32)), tl, 0), axis=1, keepdims=True)
     ur = iota((8, 128), 0)
     ucore, uj = ur >> 2, ur & 3
     udev = ((f + c * (g - f)) * 4 + g + c * (f - g)) * 2 + ucore
     own = table == udev
-    spot = (lane >> 5) * 8 + ucore * 4 + mm(one_hot(own), earlier).astype(I32)
-    turn_in = mm(one_hot(own), lower)
+    spot = (lane >> 5) * 8 + ucore * 4 + mm(one_hot(own), earlier[...]).astype(I32)
+    turn_in = mm(one_hot(own), lower[...])
     last = jnp.sum(jnp.where(own & (turn_in == uj.astype(F32)), spot, 0), axis=1, keepdims=True)
     tabv[0:32] = jnp.broadcast_to(pick, (32, 128))
     tabv[32:40] = jnp.broadcast_to(last, (8, 128))
     tcopy = pltpu.make_async_copy(tabv, tabs, lsem.at[4])
     tcopy.start()
-    tcopy.wait()
-
-    for copy in c1:
-        copy.wait_recv()
-    c2 = []
-    for j in (1, 2, 3, 0):
-        for i in range(8):
-            which = tabs[j * 8 + i, 0]
-            chosen = cand[which >> 3, (which >> 2) & 1, which & 3]
-            if j:
-                sel[j - 1, i] = chosen
-            else:
-                fin[0, i] = chosen
-        if j:
-            c2.append(send(sel.at[j - 1], fin.at[j], cs.at[3 + j], cr.at[3 + j], on_g(j)))
 
     loads[2].wait()
     w0.wait_recv()
     swaps = []
-    for j in range(4):
+    for j in (0, 1, 3, 2):
         if j:
             for grp in range(2):
                 for k in range(4):
@@ -281,9 +292,25 @@
         swaps.append(
             send(vals.at[c, pl.ds(64 * j, 64)], vals.at[c, pl.ds(64 * j, 64)], sv.at[j], rv.at[j], sibling)
         )
+
+    tcopy.wait()
+    for k, sc in ((1, 1), (3, 0), (2, 0), (2, 1)):
+        arrived(k, sc).wait_recv()
+    c2 = []
+    for j in (1, 3, 2, 0):
+        for i in range(8):
+            which = tabs[j * 8 + i, 0]
+            chosen = cand[which >> 3, (which >> 2) & 1, which & 3]
+            if j:
+                sel[j - 1, i] = chosen
+            else:
+                fin[0, i] = chosen
+        if j:
+            c2.append(send(sel.at[j - 1], fin.at[j], cs.at[3 + j], cr.at[3 + j], on_g(j)))
+
     for copy in swaps:
         copy.wait_recv()
-    flat = mm(order, vals[...].reshape(512, 512)).astype(BF)
+    flat[...] = mm(order[...], vals[...].reshape(512, 512)).astype(BF)
     loads[3].wait()
     w1.wait_recv()
 
@@ -315,12 +342,45 @@
         )
         return table[i]()
 
+    c3 = pltpu.make_async_remote_copy(
+        src_ref=swp, dst_ref=swr, send_sem=cs.at[7], recv_sem=cr.at[7],
+        device_id=sibling, device_id_type=MESH,
+    )
+    kept = [0] * MOVE
+    count = 0
+    for r in range(ROWS):
+        gone = (out_s[0] == r) | (out_s[1] == r) | (out_s[2] == r) | (out_s[3] == r)
+        stay = 1 - gone.astype(I32)
+        for j in range(MOVE):
+            kept[j] = kept[j] + jnp.where(count == j, stay * r, 0)
+        count = count + stay
+
+    def place_rows():
+        for copy in c2:
+            copy.wait_recv()
+        for j in range(MOVE):
+            there = tabs[32 + (1 - c) * 4 + j, 0]
+            here = tabs[32 + c * 4 + j, 0]
+            swp[j] = fin[there >> 3, there & 7]
+            nc_v[MOVE + j, pl.ds(mine, 32)] = fin[here >> 3, here & 7]
+        c3.start()
+        for j in range(MOVE):
+            nc_v[j] = upd[kept[j]]
+
+    def store_rows():
+        c3.wait_recv()
+        for j in range(MOVE):
+            nc_v[MOVE + j, pl.ds(theirs, 32)] = swr[j]
+
     def step(t, carry):
+        pl.when(t == SUBS - 1)(place_rows)
+        pl.when(t == SUBS + 1)(store_rows)
+
         @pl.when(t < SUBS)
         def _():
             s = t
             cols = pl.ds(pl.multiple_of(s * SUB, SUB), SUB)
-            part[s] = mm(flat, wout[:, cols]).astype(BF).reshape(4, 64, SUB)
+            part[s] = mm(flat[...], wout[:, cols]).astype(BF).reshape(4, 64, SUB)
             for i in range(4):
                 copy_of(s, i).start()
 
@@ -360,35 +420,12 @@
             for i in (8, 9, 10, 11):
                 copy_of(s, i).wait_recv()
             whole = p2[s, g].astype(F32) + ac2[s, 0].astype(F32) + ac2[s, 1].astype(F32)
-            att[s] = whole.astype(BF)
             cols = pl.ds(pl.multiple_of(s * SUB, SUB), SUB)
-            pltpu.make_async_copy(att.at[s], att_h.at[:, cols], osem.at[s]).start()
+            att_v[:, :, cols] = whole.reshape(ROWS, 2, SUB).astype(BF)
 
         return carry
 
     lax.fori_loop(0, SUBS + 4, step, 0)
-
-    for copy in c2:
-        copy.wait_recv()
-    for j in range(MOVE):
-        there = tabs[32 + (1 - c) * 4 + j, 0]
-        here = tabs[32 + c * 4 + j, 0]
-        swp[j] = fin[there >> 3, there & 7]
-        outc[MOVE + j, pl.ds(mine, 32)] = fin[here >> 3, here & 7]
-    c3 = send(swp, outc.at[pl.ds(MOVE, MOVE), pl.ds(mine, 32)], cs.at[7], cr.at[7], sibling)
-    kept = [0] * MOVE
-    count = 0
-    for r in range(ROWS):
-        gone = (out_s[0] == r) | (out_s[1] == r) | (out_s[2] == r) | (out_s[3] == r)
-        stay = 1 - gone.astype(I32)
-        for j in range(MOVE):
-            kept[j] = kept[j] + jnp.where(count == j, stay * r, 0)
-        count = count + stay
-    for j in range(MOVE):
-        outc[j] = upd[kept[j]]
-    c3.wait_recv()
-    finish = pltpu.make_async_copy(outc, nc_h, lsem.at[5])
-    finish.start()
 
     for copy in g1 + g2 + [g3, c0, w0, w1] + c1 + c2 + swaps + [c3]:
         copy.wait_send()
@@ -398,19 +435,26 @@
     def drain(s, carry):
         for i in range(12):
             copy_of(s, i).wait_send()
-        cols = pl.ds(pl.multiple_of(s * SUB, SUB), SUB)
-        pltpu.make_async_copy(att.at[s], att_h.at[:, cols], osem.at[s]).wait()
         return carry
 
     lax.fori_loop(0, SUBS, drain, 0)
-    finish.wait()
 
 
 def per_device(cache, lengths, queries, fresh, w_uv, w_out, outgoing, targets):
-    smem = pl.BlockSpec(memory_space=pltpu.SMEM)
-    hbm = pl.BlockSpec(memory_space=pl.ANY)
+    hbm = pl.BlockSpec(memory_space=pltpu.HBM)
     dma = pltpu.SemaphoreType.DMA
     scratch = [
+        pltpu.SMEM((ROWS,), I32),
+        pltpu.SMEM((MOVE,), I32),
+        pltpu.SMEM((MOVE,), I32),
+        pltpu.VMEM((ROWS, 2, ENT), BF),
+        pltpu.VMEM((512, 512), BF),
+        pltpu.VMEM((512, 512), BF),
+        pltpu.VMEM((512, 512), BF),
+        pltpu.VMEM((128, 128), BF),
+        pltpu.VMEM((128, 128), BF),
+        pltpu.VMEM((256, 512), BF),
+        pltpu.VMEM((256, 512), BF),
         pltpu.VMEM((ROWS, CAP, ENT), BF),
         pltpu.VMEM((ROWS, 128, ENT), BF),
         pltpu.VMEM((4, LAT, VD), BF),
@@ -428,16 +472,15 @@
         pltpu.VMEM((SUBS, 2, 16, HALF), BF),
         pltpu.VMEM((SUBS, 2, 16, HALF), BF),
         pltpu.VMEM((SUBS, 2, 16, SUB), BF),
-        pltpu.VMEM((SUBS, 16, SUB), BF),
         pltpu.VMEM((4, 2, MOVE, 32, ENT), BF),
         pltpu.VMEM((MOVE, 32, ENT), BF),
         pltpu.VMEM((3, 8, 32, ENT), BF),
         pltpu.VMEM((4, 8, 32, ENT), BF),
         pltpu.VMEM((MOVE, 32, ENT), BF),
-        pltpu.VMEM((ROWS, CAP, ENT), BF),
+        pltpu.VMEM((MOVE, 32, ENT), BF),
         pltpu.VMEM((40, 128), I32),
         pltpu.SMEM((40, 128), I32),
-        dma((6,)),
+        dma((10,)),
         dma((7,)), dma((7,)),
         dma((2,)), dma((2,)),
         dma((2, 3)), dma((2, 3)),
@@ -445,24 +488,25 @@
         dma((4,)), dma((4,)),
         dma((SUBS, 12)), dma((SUBS, 12)),
         dma((8,)), dma((8,)),
-        dma((SUBS,)),
+        dma((3, 2)), dma((3, 2)),
     ]
+    operands = (lengths, outgoing, targets, fresh, cache, queries.reshape(ROWS, 128, ENT), w_uv, w_out)
     new_cache, attended = pl.pallas_call(
         kernel,
         out_shape=(
-            jax.ShapeDtypeStruct((ROWS, CAP, ENT), BF),
-            jax.ShapeDtypeStruct((2 * ROWS, D), BF),
+            pltpu.VMEM((ROWS, CAP, ENT), BF),
+            pltpu.VMEM((ROWS, 2, D), BF),
         ),
-        in_specs=[smem, smem, smem, pl.BlockSpec(memory_space=pltpu.VMEM), hbm, hbm, hbm, hbm],
-        out_specs=(hbm, hbm),
+        in_specs=[hbm] * 8,
+        out_specs=(pl.BlockSpec(memory_space=pltpu.VMEM), pl.BlockSpec(memory_space=pltpu.VMEM)),
         scratch_shapes=scratch,
         compiler_params=pltpu.CompilerParams(
-            collective_id=0, has_side_effects=True, vmem_limit_bytes=48 * 1024 * 1024
+            collective_id=0, has_side_effects=True, vmem_limit_bytes=56 * 1024 * 1024
         ),
         cost_estimate=pl.CostEstimate(flops=4 * 10**9, bytes_accessed=8 * 10**6, transcendentals=10**6),
         name="mla_decode",
-    )(lengths, outgoing, targets, fresh, cache, queries.reshape(ROWS, 128, ENT), w_uv, w_out)
-    return new_cache, attended.reshape(ROWS, 2, D)
+    )(*[pltpu.with_memory_space_constraint(a, pltpu.HBM) for a in operands])
+    return new_cache, attended
 
 
 def solution(mesh):

time: 78.6 us -> 69.1 us (0.88)
  the two profiles are of different devices: /device:TPU:1 before, /device:TPU:160 now
where the time goes in v2:
time: 69.1 us; the launch traced here: 69 us
  Pallas kernels  66.8 us (97%)
  local copies, waits for them, and re-layouts  1.53 us (2%)
    pallas_call x1, Pallas kernels, per_device(): pl.pallas_call(kernel, out_shape=(pltpu.VMEM((ROWS, CAP, ENT), BF), pltpu...  66.8 us
    unnamed x2, local copies, waits for them, and re-layouts  1.53 us

profile of v2, /device:TPU:160, one launch (start us, length us, event | category | flops | bytes accessed | tf_op | source)
XLA Modules:
  0.0 69.0 jit_solution(9907220339032493345)
XLA Ops:
  0.6 66.8 %mla_decode.1 = (bf16[8,64,576]{2,1,0:T(8,128)(2,1)S(1)}, bf16[8,2,7168]{2,1,0:T(2,128)(2,1)S(1)}) custom-call(s32[8]{0:T(128)} %len_h.1, s32[4]{0:T(128)} %out_h.1, s32[4]{0:T(128)} %tgt_h.1, bf16[8,2,576]{2,1,0:T(2,128)(2,1)} %fresh_h.1, bf16[8,64,576]{2,1,0:T(8,128)(2,1)} %cache_h.1, bf16[8,128,576]{2,1,0:T(8,128)(2,1)} %bitcast.1, ...), custom_call_target="tpu_custom_call" | custom-call | flops 4000000000 | bytes 8000000 | tf_op jit(solution)/shard_map/mla_decode/pallas_call | solution.py:494
  67.5 0.8 %copy.12 = bf16[8,64,576]{2,1,0:T(8,128)(2,1)} copy(bf16[8,64,576]{2,1,0:T(8,128)(2,1)S(1)} %get-tuple-element.2) | data formatting | bytes 1179648
  68.3 0.7 copy.13

commit v3 on v2

--- a/solution.py
+++ b/solution.py
@@ -17,7 +17,8 @@
 MOVE = 4
 SUBS = 7
 SUB = D // SUBS
-HALF = SUB // 2
+AT = (0, 2, 4, 6)
+POINT = 8
 MESH = pl.DeviceIdType.MESH
 BF = jnp.bfloat16
 F32 = jnp.float32
@@ -42,7 +43,7 @@
     len_s, out_s, tgt_s, fresh_v,
     turn, before, within, earlier, lower, order, flat,
     upd, q_v, wuv, wout, lat, in1, in2, vals, gall,
-    part, rl, mg, ac, p2, rl2, mg2, ac2,
+    part, rl, mg, ac, p2, ac2,
     cand, sib, sel, fin, swp, swr, tabv, tabs,
     lsem, gsem, grec, wsem, wrec, s1, r1, s2, r2, sv, rv,
     srs, rrs, cs, cr, cks, ckr,
@@ -93,36 +94,7 @@
         pl.semaphore_signal(barrier, inc=1, device_id=on_g(k), device_id_type=MESH)
     pl.semaphore_signal(barrier, inc=1, device_id=sibling, device_id_type=MESH)
 
-    ro = iota((512, 1), 0)
-    of, og, oh, orow, ostep = ro >> 7, (ro >> 5) & 3, (ro >> 3) & 3, (ro >> 1) & 3, ro & 1
-    ox = of + c * (og - of)
-    oy = og + c * (of - og)
-    wanted = orow * 128 + ostep * 64 + (ox * 4 + oy) * 4 + oh
-    turn[...] = one_hot(iota((512, 512), 1) == wanted)
-
-    def source(l):
-        cs_, dg_, df_ = l >> 8, (l >> 6) & 3, (l >> 4) & 3
-        fs = (x + cs_ * (y - x) - df_) & 3
-        gs = (y + cs_ * (x - y) - dg_) & 3
-        return ((fs + cs_ * (gs - fs)) * 4 + gs + cs_ * (fs - gs)) * 2 + cs_
-
-    wide = iota((1, 512), 1)
-    tall = iota((512, 1), 0)
-    from_w, from_t = source(wide), source(tall)
-    slot_w, slot_t = (wide >> 1) & 7, (tall >> 1) & 7
-    even = (tall & 1) == 0
-    before[...] = one_hot(even & (from_t < from_w))
-    within[...] = one_hot(even & (from_t == from_w) & (slot_t < slot_w))
-    lt, lw = iota((128, 128), 0), iota((128, 128), 1)
     lane = iota((1, 128), 1)
-
-    def mover(l):
-        fs = (f - ((l >> 3) & 3)) & 3
-        gs = (g - (l >> 5)) & 3
-        return ((fs + c * (gs - fs)) * 4 + gs + c * (fs - gs)) * 2 + ((l >> 2) & 1)
-
-    earlier[...] = one_hot(((lt >> 5) == (lw >> 5)) & (lt < lw))
-    lower[...] = one_hot(mover(iota((128, 1), 0)) < mover(lane))
 
     small[0].wait()
     small[1].wait()
@@ -152,17 +124,22 @@
         sib[m] = upd[out_s[m], pl.ds(theirs, 32)]
         cand[0, c, m] = upd[out_s[m], pl.ds(mine, 32)]
 
+    ro = iota((512, 1), 0)
+    of, og, oh, orow, ostep = ro >> 7, (ro >> 5) & 3, (ro >> 3) & 3, (ro >> 1) & 3, ro & 1
+    ox = of + c * (og - of)
+    oy = og + c * (of - og)
+    wanted = orow * 128 + ostep * 64 + (ox * 4 + oy) * 4 + oh
+    turn[...] = one_hot(iota((512, 512), 1) == wanted)
+
+
     pl.semaphore_wait(barrier, 7)
     g1 = [send(gall.at[c, 0, 0], gall.at[c, 0, k], gsem.at[k - 1], grec.at[k - 1], on_f(k)) for k in (1, 2, 3)]
     c0 = send(sib, cand.at[0, c], cs.at[0], cr.at[0], sibling)
 
     def pass_rows(k, sc, src):
-        return send(src, cand.at[k, sc], cks.at[k - 1, sc], ckr.at[k - 1, sc], on_f(k if k != 2 else 1 + 2 * sc))
-
-    c1 = [pass_rows(k, c, cand.at[0, c]) for k in (1, 3)]
-    w0 = send(wuv_h, wuv.at[pl.ds(2 * c, 2)], wsem.at[0], wrec.at[0], sibling)
-    w1 = send(wout_h, wout.at[pl.ds(pl.multiple_of(256 * c, 256), 256)], wsem.at[1], wrec.at[1], sibling)
-
+        return send(src, cand.at[k, sc], cks.at[k - 1, sc], ckr.at[k - 1, sc], on_f(k))
+
+    c1 = [pass_rows(k, c, cand.at[0, c]) for k in (2, 1, 3)]
     qi = iota((512, 256), 0)
     ki = iota((512, 256), 1)
     same_row = (qi >> 7) == (ki >> 6)
@@ -197,33 +174,68 @@
             l1[grp, k] = send(lat.at[grp, (f + k) % 4], in1.at[grp, k], s1.at[grp, k - 1], r1.at[grp, k - 1], on_f(k))
         onward(grp, 0, lat.at[grp, f])
         in2[0, 0, grp] = lat[grp, f, g]
-
-    c0.wait_recv()
-    c1 += [pass_rows(k, 1 - c, cand.at[0, 1 - c]) for k in (1, 3)]
+        if grp == 0:
+            c0.wait_recv()
+            c1 += [pass_rows(k, 1 - c, cand.at[0, 1 - c]) for k in (2, 1, 3)]
+
+    w0 = send(wuv_h, wuv.at[pl.ds(2 * c, 2)], wsem.at[0], wrec.at[0], sibling)
+    w1 = send(wout_h, wout.at[pl.ds(pl.multiple_of(256 * c, 256), 256)], wsem.at[1], wrec.at[1], sibling)
+
+    def source(l):
+        cs_, dg_, df_ = l >> 8, (l >> 6) & 3, (l >> 4) & 3
+        fs = (x + cs_ * (y - x) - df_) & 3
+        gs = (y + cs_ * (x - y) - dg_) & 3
+        return ((fs + cs_ * (gs - fs)) * 4 + gs + cs_ * (fs - gs)) * 2 + cs_
+
+    wide = iota((1, 512), 1)
+    tall = iota((512, 1), 0)
+    from_w, from_t = source(wide), source(tall)
+    slot_w, slot_t = (wide >> 1) & 7, (tall >> 1) & 7
+    even = (tall & 1) == 0
+    before[...] = one_hot(even & (from_t < from_w))
+    within[...] = one_hot(even & (from_t == from_w) & (slot_t < slot_w))
+    lt, lw = iota((128, 128), 0), iota((128, 128), 1)
+
+    def mover(l):
+        fs = (f - ((l >> 3) & 3)) & 3
+        gs = (g - (l >> 5)) & 3
+        return ((fs + c * (gs - fs)) * 4 + gs + c * (fs - gs)) * 2 + ((l >> 2) & 1)
+
+    earlier[...] = one_hot(((lt >> 5) == (lw >> 5)) & (lt < lw))
+    lower[...] = one_hot(mover(iota((128, 1), 0)) < mover(lane))
+
     for copy in g1:
         copy.wait_recv()
     g2 = [send(gall.at[c, 0], gall.at[c, k], gsem.at[2 + k], grec.at[2 + k], on_g(k)) for k in (1, 2, 3)]
 
-    for grp in range(2):
+    def arrived(k, sc):
+        return pltpu.make_async_remote_copy(
+            src_ref=cand.at[0, 0], dst_ref=cand.at[k, sc], send_sem=cks.at[k - 1, sc], recv_sem=ckr.at[k - 1, sc],
+            device_id=on_f(1), device_id_type=MESH,
+        )
+
+    kept = [0] * MOVE
+    count = 0
+    for r in range(ROWS):
+        gone = (out_s[0] == r) | (out_s[1] == r) | (out_s[2] == r) | (out_s[3] == r)
+        stay = 1 - gone.astype(I32)
+        for j in range(MOVE):
+            kept[j] = kept[j] + jnp.where(count == j, stay * r, 0)
+        count = count + stay
+    for j in range(MOVE):
+        nc_v[j] = upd[kept[j]]
+
+    for copy in g2:
+        copy.wait_recv()
+    g3 = send(gall.at[c], gall.at[c], gsem.at[6], grec.at[6], sibling)
+
+    def turn_corner(grp):
         for k in (1, 3, 2):
             l1[grp, k].wait_recv()
             onward(grp, k, in1.at[grp, k])
             in2[0, k, grp] = in1[grp, k, g]
 
-    for copy in g2:
-        copy.wait_recv()
-    g3 = send(gall.at[c], gall.at[c], gsem.at[6], grec.at[6], sibling)
-
-    def arrived(k, sc):
-        return pltpu.make_async_remote_copy(
-            src_ref=cand.at[0, 0], dst_ref=cand.at[k, sc], send_sem=cks.at[k - 1, sc], recv_sem=ckr.at[k - 1, sc],
-            device_id=on_f(k if k != 2 else 1 + 2 * sc), device_id_type=MESH,
-        )
-
-    arrived(1, 0).wait_recv()
-    c1.append(pass_rows(2, 0, cand.at[1, 0]))
-    arrived(3, 1).wait_recv()
-    c1.append(pass_rows(2, 1, cand.at[3, 1]))
+    turn_corner(0)
 
     nr = iota((256, 1), 0)
     nf, ng = nr >> 6, (nr >> 4) & 3
@@ -277,8 +289,34 @@
     tcopy = pltpu.make_async_copy(tabv, tabs, lsem.at[4])
     tcopy.start()
 
+    turn_corner(1)
+
     loads[2].wait()
     w0.wait_recv()
+    def leg(j):
+        return pltpu.make_async_remote_copy(
+            src_ref=sel.at[j - 1], dst_ref=fin.at[j], send_sem=cs.at[3 + j], recv_sem=cr.at[3 + j],
+            device_id=on_g(j), device_id_type=MESH,
+        )
+
+    def select_rows(legs):
+        for j in legs:
+            for i in range(8):
+                which = tabs[j * 8 + i, 0]
+                chosen = cand[which >> 3, (which >> 2) & 1, which & 3]
+                if j:
+                    sel[j - 1, i] = chosen
+                else:
+                    fin[0, i] = chosen
+            if j:
+                leg(j).start()
+
+    tcopy.wait()
+    for k in (1, 2, 3):
+        for sc in range(2):
+            arrived(k, sc).wait_recv()
+    select_rows((1, 3, 2, 0))
+
     swaps = []
     for j in (0, 1, 3, 2):
         if j:
@@ -293,21 +331,6 @@
             send(vals.at[c, pl.ds(64 * j, 64)], vals.at[c, pl.ds(64 * j, 64)], sv.at[j], rv.at[j], sibling)
         )
 
-    tcopy.wait()
-    for k, sc in ((1, 1), (3, 0), (2, 0), (2, 1)):
-        arrived(k, sc).wait_recv()
-    c2 = []
-    for j in (1, 3, 2, 0):
-        for i in range(8):
-            which = tabs[j * 8 + i, 0]
-            chosen = cand[which >> 3, (which >> 2) & 1, which & 3]
-            if j:
-                sel[j - 1, i] = chosen
-            else:
-                fin[0, i] = chosen
-        if j:
-            c2.append(send(sel.at[j - 1], fin.at[j], cs.at[3 + j], cr.at[3 + j], on_g(j)))
-
     for copy in swaps:
         copy.wait_recv()
     flat[...] = mm(order[...], vals[...].reshape(512, 512)).astype(BF)
@@ -317,7 +340,6 @@
     f1, f2, f3 = (f + 1) % 4, (f + 2) % 4, (f + 3) % 4
     h1, h2, h3 = (g + 1) % 4, (g + 2) % 4, (g + 3) % 4
     low, high = pl.ds(0, 32), pl.ds(32, 32)
-    left, right = pl.ds(0, HALF), pl.ds(HALF, HALF)
 
     def rs(s, i, src, dst, device):
         return pltpu.make_async_remote_copy(
@@ -333,12 +355,9 @@
             lambda: rs(s, 3, part.at[s, f3, low], ac.at[s, 1, low], on_f(3)),
             lambda: rs(s, 4, mg.at[s, 0], ac.at[s, 0, low], on_f(1)),
             lambda: rs(s, 5, mg.at[s, 1], ac.at[s, 1, high], on_f(3)),
-            lambda: rs(s, 6, p2.at[s, h2, :, left], rl2.at[s, 0], on_g(1)),
-            lambda: rs(s, 7, p2.at[s, h2, :, right], rl2.at[s, 1], on_g(3)),
-            lambda: rs(s, 8, p2.at[s, h1, :, right], ac2.at[s, 0, :, right], on_g(1)),
-            lambda: rs(s, 9, p2.at[s, h3, :, left], ac2.at[s, 1, :, left], on_g(3)),
-            lambda: rs(s, 10, mg2.at[s, 0], ac2.at[s, 0, :, left], on_g(1)),
-            lambda: rs(s, 11, mg2.at[s, 1], ac2.at[s, 1, :, right], on_g(3)),
+            lambda: rs(s, 6, p2.at[s, h1], ac2.at[s, 0], on_g(1)),
+            lambda: rs(s, 7, p2.at[s, h2], ac2.at[s, 1], on_g(2)),
+            lambda: rs(s, 8, p2.at[s, h3], ac2.at[s, 2], on_g(3)),
         )
         return table[i]()
 
@@ -346,26 +365,15 @@
         src_ref=swp, dst_ref=swr, send_sem=cs.at[7], recv_sem=cr.at[7],
         device_id=sibling, device_id_type=MESH,
     )
-    kept = [0] * MOVE
-    count = 0
-    for r in range(ROWS):
-        gone = (out_s[0] == r) | (out_s[1] == r) | (out_s[2] == r) | (out_s[3] == r)
-        stay = 1 - gone.astype(I32)
-        for j in range(MOVE):
-            kept[j] = kept[j] + jnp.where(count == j, stay * r, 0)
-        count = count + stay
-
     def place_rows():
-        for copy in c2:
-            copy.wait_recv()
+        for j in (1, 2, 3):
+            leg(j).wait_recv()
         for j in range(MOVE):
             there = tabs[32 + (1 - c) * 4 + j, 0]
             here = tabs[32 + c * 4 + j, 0]
             swp[j] = fin[there >> 3, there & 7]
             nc_v[MOVE + j, pl.ds(mine, 32)] = fin[here >> 3, here & 7]
         c3.start()
-        for j in range(MOVE):
-            nc_v[j] = upd[kept[j]]
 
     def store_rows():
         c3.wait_recv()
@@ -373,8 +381,6 @@
             nc_v[MOVE + j, pl.ds(theirs, 32)] = swr[j]
 
     def step(t, carry):
-        pl.when(t == SUBS - 1)(place_rows)
-        pl.when(t == SUBS + 1)(store_rows)
 
         @pl.when(t < SUBS)
         def _():
@@ -384,9 +390,9 @@
             for i in range(4):
                 copy_of(s, i).start()
 
-        @pl.when((t >= 1) & (t < SUBS + 1))
+        @pl.when((t >= AT[1]) & (t < SUBS + AT[1]))
         def _():
-            s = t - 1
+            s = t - AT[1]
             copy_of(s, 0).wait_recv()
             mg[s, 0] = (part[s, f1, low].astype(F32) + rl[s, 0].astype(F32)).astype(BF)
             copy_of(s, 4).start()
@@ -394,46 +400,40 @@
             mg[s, 1] = (part[s, f3, high].astype(F32) + rl[s, 1].astype(F32)).astype(BF)
             copy_of(s, 5).start()
 
-        @pl.when((t >= 2) & (t < SUBS + 2))
+        @pl.when((t >= AT[2]) & (t < SUBS + AT[2]))
         def _():
-            s = t - 2
+            s = t - AT[2]
             for i in (2, 3, 4, 5):
                 copy_of(s, i).wait_recv()
             whole = part[s, f].astype(F32) + ac[s, 0].astype(F32) + ac[s, 1].astype(F32)
             p2[s] = whole.astype(BF).reshape(4, 16, SUB)
-            for i in (6, 7, 8, 9):
+            for i in (7, 6, 8):
                 copy_of(s, i).start()
 
-        @pl.when((t >= 3) & (t < SUBS + 3))
+        @pl.when(t >= AT[3])
         def _():
-            s = t - 3
-            copy_of(s, 6).wait_recv()
-            mg2[s, 0] = (p2[s, h1, :, left].astype(F32) + rl2[s, 0].astype(F32)).astype(BF)
-            copy_of(s, 10).start()
-            copy_of(s, 7).wait_recv()
-            mg2[s, 1] = (p2[s, h3, :, right].astype(F32) + rl2[s, 1].astype(F32)).astype(BF)
-            copy_of(s, 11).start()
-
-        @pl.when(t >= 4)
-        def _():
-            s = t - 4
-            for i in (8, 9, 10, 11):
+            s = t - AT[3]
+            for i in (6, 7, 8):
                 copy_of(s, i).wait_recv()
-            whole = p2[s, g].astype(F32) + ac2[s, 0].astype(F32) + ac2[s, 1].astype(F32)
+            whole = p2[s, g].astype(F32)
+            for i in range(3):
+                whole = whole + ac2[s, i].astype(F32)
             cols = pl.ds(pl.multiple_of(s * SUB, SUB), SUB)
             att_v[:, :, cols] = whole.reshape(ROWS, 2, SUB).astype(BF)
 
+        pl.when(t == POINT)(place_rows)
+        pl.when(t == POINT + 2)(store_rows)
         return carry
 
-    lax.fori_loop(0, SUBS + 4, step, 0)
-
-    for copy in g1 + g2 + [g3, c0, w0, w1] + c1 + c2 + swaps + [c3]:
+    lax.fori_loop(0, SUBS + AT[3], step, 0)
+
+    for copy in g1 + g2 + [g3, c0, w0, w1] + c1 + [leg(1), leg(2), leg(3)] + swaps + [c3]:
         copy.wait_send()
     for copy in list(l1.values()) + list(l2.values()):
         copy.wait_send()
 
     def drain(s, carry):
-        for i in range(12):
+        for i in range(9):
             copy_of(s, i).wait_send()
         return carry
 
@@ -469,9 +469,7 @@
         pltpu.VMEM((SUBS, 2, 32, SUB), BF),
         pltpu.VMEM((SUBS, 2, 64, SUB), BF),
         pltpu.VMEM((SUBS, 4, 16, SUB), BF),
-        pltpu.VMEM((SUBS, 2, 16, HALF), BF),
-        pltpu.VMEM((SUBS, 2, 16, HALF), BF),
-        pltpu.VMEM((SUBS, 2, 16, SUB), BF),
+        pltpu.VMEM((SUBS, 3, 16, SUB), BF),
         pltpu.VMEM((4, 2, MOVE, 32, ENT), BF),
         pltpu.VMEM((MOVE, 32, ENT), BF),
         pltpu.VMEM((3, 8, 32, ENT), BF),
@@ -486,7 +484,7 @@
         dma((2, 3)), dma((2, 3)),
         dma((2, 4, 3)), dma((2, 4, 3)),
         dma((4,)), dma((4,)),
-        dma((SUBS, 12)), dma((SUBS, 12)),
+        dma((SUBS, 9)), dma((SUBS, 9)),
         dma((8,)), dma((8,)),
         dma((3, 2)), dma((3, 2)),
     ]

time: 69.1 us -> 64.3 us (0.931)
  the two profiles are of different devices: /device:TPU:160 before, /device:TPU:1 now
where the time goes in v3:
time: 64.3 us; the launch traced here: 64.2 us
  Pallas kernels  62.1 us (97%)
  local copies, waits for them, and re-layouts  1.53 us (2%)
    pallas_call x1, Pallas kernels, per_device(): pl.pallas_call(kernel, out_shape=(pltpu.VMEM((ROWS, CAP, ENT), BF), pltpu...  62.1 us
    unnamed x2, local copies, waits for them, and re-layouts  1.53 us

profile of v3, /device:TPU:1, one launch (start us, length us, event | category | flops | bytes accessed | tf_op | source)
XLA Modules:
  0.0 64.2 jit_solution(15320461931706060641)
XLA Ops:
  0.6 62.1 %mla_decode.1 = (bf16[8,64,576]{2,1,0:T(8,128)(2,1)S(1)}, bf16[8,2,7168]{2,1,0:T(2,128)(2,1)S(1)}) custom-call(s32[8]{0:T(128)} %len_h.1, s32[4]{0:T(128)} %out_h.1, s32[4]{0:T(128)} %tgt_h.1, bf16[8,2,576]{2,1,0:T(2,128)(2,1)} %fresh_h.1, bf16[8,64,576]{2,1,0:T(8,128)(2,1)} %cache_h.1, bf16[8,128,576]{2,1,0:T(8,128)(2,1)} %bitcast.1, ...), custom_call_target="tpu_custom_call" | custom-call | flops 4000000000 | bytes 8000000 | tf_op jit(solution)/shard_map/mla_decode/pallas_call | solution.py:492
  62.7 0.8 %copy.12 = bf16[8,64,576]{2,1,0:T(8,128)(2,1)} copy(bf16[8,64,576]{2,1,0:T(8,128)(2,1)S(1)} %get-tuple-element.2) | data formatting | bytes 1179648
  63.6 0.7 %copy.13 = bf16[8,2,7168]{2,1,0:T(2,128)(2,1)} copy(bf16[8,2,7168]{2,1,0:T(2,128)(2,1)S(1)} %get-tuple-element.3) | data formatting | bytes 458752

commit v4 on v3

--- a/solution.py
+++ b/solution.py
@@ -315,7 +315,7 @@
     for k in (1, 2, 3):
         for sc in range(2):
             arrived(k, sc).wait_recv()
-    select_rows((1, 3, 2, 0))
+    select_rows((2, 1, 3, 0))
 
     swaps = []
     for j in (0, 1, 3, 2):

time: 64.3 us -> 63.6 us (0.989)
  Pallas kernels: 62.1 us -> 61.3 us
    pallas_call x1, Pallas kernels: 62.1 us -> 61.3 us  [per_device(): pl.pallas_call(kernel, out_shape=(pltpu.VMEM((ROWS, CAP, ENT), BF), pltpu...]
where the time goes in v4:
time: 63.6 us; the launch traced here: 63.5 us
  Pallas kernels  61.3 us (96%)
  local copies, waits for them, and re-layouts  1.53 us (2%)
  between operations  0.64 us (1%)
    pallas_call x1, Pallas kernels, per_device(): pl.pallas_call(kernel, out_shape=(pltpu.VMEM((ROWS, CAP, ENT), BF), pltpu...  61.3 us
    unnamed x2, local copies, waits for them, and re-layouts  1.53 us

profile of v4, /device:TPU:1, one launch (start us, length us, event | category | flops | bytes accessed | tf_op | source)
XLA Modules:
  0.0 63.5 jit_solution(3877946808124715035)
XLA Ops:
  0.6 61.3 %mla_decode.1 = (bf16[8,64,576]{2,1,0:T(8,128)(2,1)S(1)}, bf16[8,2,7168]{2,1,0:T(2,128)(2,1)S(1)}) custom-call(s32[8]{0:T(128)} %len_h.1, s32[4]{0:T(128)} %out_h.1, s32[4]{0:T(128)} %tgt_h.1, bf16[8,2,576]{2,1,0:T(2,128)(2,1)} %fresh_h.1, bf16[8,64,576]{2,1,0:T(8,128)(2,1)} %cache_h.1, bf16[8,128,576]{2,1,0:T(8,128)(2,1)} %bitcast.1, ...), custom_call_target="tpu_custom_call" | custom-call | flops 4000000000 | bytes 8000000 | tf_op jit(solution)/shard_map/mla_decode/pallas_call | solution.py:492
  61.9 0.8 %copy.12 = bf16[8,64,576]{2,1,0:T(8,128)(2,1)} copy(bf16[8,64,576]{2,1,0:T(8,128)(2,1)S(1)} %get-tuple-element.2) | data formatting | bytes 1179648
  62.8 0.7 %copy.13 = bf16[8,2,7168]{2,1,0:T(2,128)(2,1)} copy(bf16[8,2,7168]{2,1,0:T(2,128)(2,1)S(1)} %get-tuple-element.3) | data formatting | bytes 458752

commit v5 on v4

--- a/solution.py
+++ b/solution.py
@@ -170,7 +170,7 @@
         turned = mm(turn[...], probs).astype(BF)
         latent = mm(turned, keys[:, :LAT]).astype(BF)
         lat[grp] = latent.reshape(4, 4, 32, LAT)
-        for k in (2, 1, 3):
+        for k in (1, 3, 2):
             l1[grp, k] = send(lat.at[grp, (f + k) % 4], in1.at[grp, k], s1.at[grp, k - 1], r1.at[grp, k - 1], on_f(k))
         onward(grp, 0, lat.at[grp, f])
         in2[0, 0, grp] = lat[grp, f, g]
@@ -331,9 +331,12 @@
             send(vals.at[c, pl.ds(64 * j, 64)], vals.at[c, pl.ds(64 * j, 64)], sv.at[j], rv.at[j], sibling)
         )
 
+    ours = pl.ds(pl.multiple_of(256 * c, 256), 256)
+    others = pl.ds(pl.multiple_of(256 * (1 - c), 256), 256)
+    kept_rows = mm(order[:, ours], vals[c])
     for copy in swaps:
         copy.wait_recv()
-    flat[...] = mm(order[...], vals[...].reshape(512, 512)).astype(BF)
+    flat[...] = (kept_rows + mm(order[:, others], vals[1 - c])).astype(BF)
     loads[3].wait()
     w1.wait_recv()
 

time: 63.6 us -> 63.3 us (level)
  no operation moved by 1% of the time
where the time goes in v5:
time: 63.3 us; the launch traced here: 63.2 us
  Pallas kernels  61.1 us (97%)
  local copies, waits for them, and re-layouts  1.53 us (2%)
  between operations  0.64 us (1%)
    pallas_call x1, Pallas kernels, per_device(): pl.pallas_call(kernel, out_shape=(pltpu.VMEM((ROWS, CAP, ENT), BF), pltpu...  61.1 us
    unnamed x2, local copies, waits for them, and re-layouts  1.53 us

profile of v5, /device:TPU:1, one launch (start us, length us, event | category | flops | bytes accessed | tf_op | source)
XLA Modules:
  0.0 63.2 jit_solution(10887550998358022219)
XLA Ops:
  0.6 61.1 %mla_decode.1 = (bf16[8,64,576]{2,1,0:T(8,128)(2,1)S(1)}, bf16[8,2,7168]{2,1,0:T(2,128)(2,1)S(1)}) custom-call(s32[8]{0:T(128)} %len_h.1, s32[4]{0:T(128)} %out_h.1, s32[4]{0:T(128)} %tgt_h.1, bf16[8,2,576]{2,1,0:T(2,128)(2,1)} %fresh_h.1, bf16[8,64,576]{2,1,0:T(8,128)(2,1)} %cache_h.1, bf16[8,128,576]{2,1,0:T(8,128)(2,1)} %bitcast.1, ...), custom_call_target="tpu_custom_call" | custom-call | flops 4000000000 | bytes 8000000 | tf_op jit(solution)/shard_map/mla_decode/pallas_call | solution.py:495
  61.7 0.8 %copy.12 = bf16[8,64,576]{2,1,0:T(8,128)(2,1)} copy(bf16[8,64,576]{2,1,0:T(8,128)(2,1)S(1)} %get-tuple-element.2) | data formatting | bytes 1179648
  62.5 0.7 %copy.13 = bf16[8,2,7168]{2,1,0:T(2,128)(2,1)} copy(bf16[8,2,7168]{2,1,0:T(2,128)(2,1)S(1)} %get-tuple-element.3) | data formatting | bytes 458752
